TPU v7x, 128 devices: a whole 4x4x4 slice. The times are simulated.
128 devices in a mesh: width: 8 (over y_lo, z), hidden: 16 (over x, y_hi, core).
Axes of the slice: x: 4, y: 4 (y_hi: 2, y_lo: 2; y = y_hi * 2 + y_lo), z: 4, core: 2. Of those that a mesh axis runs over, the one named last changes fastest.
Arguments:
- tokens: bfloat16 [768, 8192], P('hidden', 'width'), may hold values from -6 to 6
- gate_weight: bfloat16 [8192, 28672], P('width', 'hidden'), may hold values from -0.09375 to 0.09375
- up_weight: bfloat16 [8192, 28672], P('width', 'hidden'), may hold values from -0.09375 to 0.09375
- down_weight: bfloat16 [28672, 8192], P('hidden', 'width'), may hold values from -0.046875 to 0.046875
- grad_out: bfloat16 [768, 8192], P('hidden', 'width'), may hold values from -6 to 6
- pattern_gate: int32 [64, 112], P('width'), may hold values from 0 to 223, all different within a row
- pattern_up: int32 [64, 112], P('width'), may hold values from 0 to 223, all different within a row
- pattern_down: int32 [224, 32], P('hidden'), may hold values from 0 to 63, all different within a row
Outputs:
- output: bfloat16 [768, 8192], P('hidden', 'width')
- grad_tokens: bfloat16 [768, 8192], P('hidden', 'width')
- grad_gate: bfloat16 [8192, 28672], P('width', 'hidden')
- grad_up: bfloat16 [8192, 28672], P('width', 'hidden')
- grad_down: bfloat16 [28672, 8192], P('hidden', 'width')
Inputs may be any that keep to these rules, and one draw needn't show every extreme that they name: `pattern_gate`: each row names 112 distinct block columns, and every block column is named by some row. `pattern_up`: each row names 112 distinct block columns, and every block column is named by some row. `pattern_down`: each row names 32 distinct block columns, and every block column is named by some row.
All inputs are finite; a program needn't handle non-finite values.
Results may differ from a plain program's by a relative error of at most 0.005.
Values may be sent and summed in bfloat16 or wider, within the bound.
A program may use at most 128 MiB of HBM per device.

v0:
```python
import jax
import jax.numpy as jnp
from jax import lax
from jax.sharding import PartitionSpec as P

BLOCK = 128


def block_mask(pattern, first, count):
    columns = first + jnp.arange(count, dtype=jnp.int32)
    hit = jnp.any(pattern[:, :, None] == columns[None, None, :], axis=1)
    return jnp.repeat(jnp.repeat(hit, BLOCK, axis=0), BLOCK, axis=1)


def per_device(
    tokens, gate_weight, up_weight, down_weight, grad_out, pattern_gate, pattern_up, pattern_down
):
    hidden_index = lax.axis_index("hidden")
    width_index = lax.axis_index("width")
    local_width = gate_weight.shape[0]
    local_hidden = gate_weight.shape[1]
    zero = jnp.zeros((), jnp.bfloat16)
    hidden_blocks = local_hidden // BLOCK
    width_blocks = local_width // BLOCK
    mask_gate = block_mask(pattern_gate, hidden_index * hidden_blocks, hidden_blocks)
    mask_up = block_mask(pattern_up, hidden_index * hidden_blocks, hidden_blocks)
    mask_down = block_mask(pattern_down, width_index * width_blocks, width_blocks)
    w_gate = jnp.where(mask_gate, gate_weight, zero)
    w_up = jnp.where(mask_up, up_weight, zero)
    w_down = jnp.where(mask_down, down_weight, zero)
    back = (((1,), (1,)), ((), ()))
    contract = (((0,), (0,)), ((), ()))
    tokens_all = lax.all_gather(tokens, "hidden", axis=0, tiled=True)
    grad_all = lax.all_gather(grad_out, "hidden", axis=0, tiled=True)
    picked = tokens_all
    both = lax.psum_scatter(
        jnp.concatenate(
            [
                jnp.dot(picked, w_gate, preferred_element_type=jnp.float32),
                jnp.dot(picked, w_up, preferred_element_type=jnp.float32),
            ],
            axis=1,
        ),
        "width",
        scatter_dimension=0,
        tiled=True,
    )
    gate = both[:, :local_hidden]
    up = both[:, local_hidden:]
    hidden = (jax.nn.silu(gate) * up).astype(jnp.bfloat16)
    hidden_all = lax.all_gather(hidden, "width", axis=0, tiled=True)
    picked = grad_all
    grad_hidden = lax.psum_scatter(
        lax.dot_general(picked, w_down, back, preferred_element_type=jnp.float32),
        "width",
        scatter_dimension=0,
        tiled=True,
    )
    sig = jax.nn.sigmoid(gate)
    d_gate = (grad_hidden * up * sig * (1.0 + gate * (1.0 - sig))).astype(jnp.bfloat16)
    d_up = (grad_hidden * gate * sig).astype(jnp.bfloat16)
    d_gate, d_up = (d_gate, d_up)
    d_gate_all, d_up_all = (
        lax.all_gather(d_gate, "width", axis=0, tiled=True),
        lax.all_gather(d_up, "width", axis=0, tiled=True),
    )
    output = lax.psum_scatter(
        jnp.dot(hidden_all, w_down, preferred_element_type=jnp.float32),
        "hidden",
        scatter_dimension=0,
        tiled=True,
    ).astype(jnp.bfloat16)
    grad_down = jnp.where(
        mask_down,
        lax.dot_general(hidden_all, grad_all, contract, preferred_element_type=jnp.float32),
        0.0,
    ).astype(jnp.bfloat16)
    grad_gate = jnp.where(
        mask_gate,
        lax.dot_general(tokens_all, d_gate_all, contract, preferred_element_type=jnp.float32),
        0.0,
    ).astype(jnp.bfloat16)
    grad_up = jnp.where(
        mask_up,
        lax.dot_general(tokens_all, d_up_all, contract, preferred_element_type=jnp.float32),
        0.0,
    ).astype(jnp.bfloat16)
    first = lax.dot_general(d_gate_all, w_gate, back, preferred_element_type=jnp.float32)
    grad_tokens = lax.psum_scatter(
        first + lax.dot_general(d_up_all, w_up, back, preferred_element_type=jnp.float32),
        "hidden",
        scatter_dimension=0,
        tiled=True,
    ).astype(jnp.bfloat16)
    return (output, grad_tokens, grad_gate, grad_up, grad_down)


def solution(mesh):
    placed = (
        P("hidden", "width"),
        P("width", "hidden"),
        P("width", "hidden"),
        P("hidden", "width"),
        P("hidden", "width"),
        P("width", None),
        P("width", None),
        P("hidden", None),
    )
    return jax.shard_map(
        per_device,
        mesh=mesh,
        in_specs=placed,
        out_specs=(
            P("hidden", "width"),
            P("hidden", "width"),
            P("width", "hidden"),
            P("width", "hidden"),
            P("hidden", "width"),
        ),
        check_vma=False,
    )
```

profile of v0, /device:TPU:1, one launch (start us, length us, event | category | flops | bytes accessed | tf_op | source)
XLA Modules:
  0.0 589.9 jit_solution(16550526613238077310)
XLA Ops:
  7.2 0.7 all-gather.10.cloned.1.call-update
  7.9 0.0 all-gather.6.cloned.1.call-start
  7.9 0.7 all-gather.6.cloned.1.call-update
  8.6 0.0 reduce-scatter.15.cloned.1.call-start
  8.7 1.1 compare_reduce_fusion
  9.8 50.9 %all-gather.10.cloned.1.call-done = bf16[768,1024]{1,0:T(8,128)(2,1)} async-done(((bf16[48,1024]{1,0:T(8,128)(2,1)}), bf16[768,1024]{1,0:T(8,128)(2,1)}) %all-gather.10.cloned.1.call-update) | async-done | bytes 1572880 | tf_op jit(solution)/shard_map/all_gather | solution.py:34
  60.7 0.1 broadcast_in_dim.47
  60.8 5.6 broadcast_in_dim.48
  66.4 8.2 %convolution_bitcast_fusion = f32[768,1792]{0,1:T(8,128)} fusion(bf16[768,1024]{1,0:T(8,128)(2,1)} %all-gather.10.cloned.1.call-done, bf16[1792,1024]{1,0:T(8,128)(2,1)} %param.11, pred[224,8,8,128]{3,2,1,0:T(8,128)(4,1)S(1)} %bitcast.57), kind=kOutput, calls=%fused_computation.9 | convolution fusion | flops 2820407296 | bytes 12582912 | tf_op jit(solution)/shard_map/dot_general | solution.py:54
  74.6 6.2 %copy.41 = f32[768,1792]{1,0:T(8,128)} copy(f32[768,1792]{0,1:T(8,128)} %convolution_bitcast_fusion) | data formatting | bytes 11010048
  80.8 0.0 reduce-scatter.13.cloned.1.call-start
  80.8 0.6 copy-done.2
  81.4 0.6 compare_reduce_fusion.2
  82.1 0.1 broadcast_bitcast_fusion
  82.2 5.9 %copy.32 = bf16[1024,1792]{0,1:T(8,128)(2,1)} copy(bf16[1024,1792]{1,0:T(8,128)(2,1)} %param.10) | data formatting | bytes 7340032 | tf_op args[2]
  88.2 5.9 %copy.31 = bf16[1024,1792]{0,1:T(8,128)(2,1)} copy(bf16[1024,1792]{1,0:T(8,128)(2,1)} %param.9) | data formatting | bytes 7340032 | tf_op args[1]
  94.1 4.3 bitcast_select_fusion.1
  98.4 2.1 bitcast_select_fusion.3
  100.5 8.1 %all-gather.6.cloned.1.call-done = bf16[768,1024]{1,0:T(8,128)(2,1)} async-done(((bf16[48,1024]{1,0:T(8,128)(2,1)}), bf16[768,1024]{1,0:T(8,128)(2,1)}) %all-gather.6.cloned.1.call-update) | async-done | bytes 1572880 | tf_op jit(solution)/shard_map/all_gather | solution.py:33
  108.6 8.1 %convolution_bitcast_fusion.1 = f32[768,1792]{0,1:T(8,128)} fusion(bf16[1024,1792]{0,1:T(8,128)(2,1)} %bitcast_select_fusion.1, bf16[768,1024]{1,0:T(8,128)(2,1)} %all-gather.6.cloned.1.call-done), kind=kOutput, calls=%fused_computation.10 | convolution fusion | flops 2818572288 | bytes 10747904 | tf_op jit(solution)/shard_map/dot_general | solution.py:40
  116.7 4.9 convolution_bitcast_fusion.2
  121.6 9.1 %pad_maximum_fusion = f32[768,3584]{0,1:T(8,128)} fusion(f32[768,1792]{0,1:T(8,128)} %convolution_bitcast_fusion.1, f32[768,1792]{0,1:T(8,128)} %convolution_bitcast_fusion.2), kind=kLoop, calls=%fused_computation | loop fusion | flops 2752512 | bytes 22020096 | tf_op jit(solution)/shard_map/concatenate | solution.py:37
  130.7 12.2 %copy.39 = f32[768,3584]{1,0:T(8,128)} copy(f32[768,3584]{0,1:T(8,128)} %pad_maximum_fusion) | data formatting | bytes 22020096
  142.9 0.0 all-gather.12.cloned.1.call-start
  142.9 32.3 %reduce-scatter.15.cloned.1.call-done = f32[96,1792]{1,0:T(8,128)} async-done(((f32[768,1792]{1,0:T(8,128)}), f32[96,1792]{1,0:T(8,128)}) %reduce-scatter.15.cloned.1.call-update) | async-done | bytes 688144 | tf_op jit(solution)/shard_map/reduce_scatter | solution.py:53
  175.2 118.6 %reduce-scatter.13.cloned.1.call-done = f32[96,3584]{1,0:T(8,128)} async-done(((f32[768,3584]{1,0:T(8,128)}), f32[96,3584]{1,0:T(8,128)}) %reduce-scatter.13.cloned.1.call-update) | async-done | bytes 1376272 | tf_op jit(solution)/shard_map/reduce_scatter | solution.py:36
  293.8 2.8 multiply_convert_fusion
  296.6 0.0 all-gather.14.cloned.1.call-start
  296.7 0.5 all-gather.14.cloned.1.call-update
  297.2 0.0 all-gather.8.cloned.1.call-start
  297.2 0.7 all-gather.8.cloned.1.call-update
  298.0 0.2 reduce-scatter.11.cloned.1.call-start
  298.2 37.2 %all-gather.12.cloned.1.call-done = bf16[768,1792]{1,0:T(8,128)(2,1)} async-done(((bf16[96,1792]{1,0:T(8,128)(2,1)}), bf16[768,1792]{1,0:T(8,128)(2,1)}) %all-gather.12.cloned.1.call-update) | async-done | bytes 2752528 | tf_op jit(solution)/shard_map/all_gather | solution.py:64
  335.4 7.5 %fusion.7 = f32[768,1024]{1,0:T(8,128)} fusion(bf16[768,1792]{1,0:T(8,128)(2,1)} %all-gather.12.cloned.1.call-done, bf16[1024,1792]{0,1:T(8,128)(2,1)} %bitcast_select_fusion.3), kind=kOutput, calls=%fused_computation.29 | convolution fusion | flops 2818572288 | bytes 9568256 | tf_op jit(solution)/shard_map/dot_general | solution.py:88
  342.9 36.3 %all-gather.14.cloned.1.call-done = bf16[768,1792]{1,0:T(8,128)(2,1)} async-done(((bf16[96,1792]{1,0:T(8,128)(2,1)}), bf16[768,1792]{1,0:T(8,128)(2,1)}) %all-gather.14.cloned.1.call-update) | async-done | bytes 2752528 | tf_op jit(solution)/shard_map/all_gather | solution.py:65
  379.2 8.4 %convolution_add_fusion = f32[768,1024]{1,0:T(8,128)} fusion(f32[768,1024]{1,0:T(8,128)} %fusion.7, bf16[768,1792]{1,0:T(8,128)(2,1)} %all-gather.14.cloned.1.call-done, bf16[1024,1792]{0,1:T(8,128)(2,1)} %bitcast_select_fusion.1), kind=kOutput, calls=%fused_computation.15 | convolution fusion | flops 2819358720 | bytes 12713984 | tf_op jit(solution)/shard_map/dot_general | solution.py:90
  387.7 0.0 reduce-scatter.9.cloned.1.call-start
  387.7 35.4 %all-gather.8.cloned.1.call-done = bf16[768,1792]{1,0:T(8,128)(2,1)} async-done(((bf16[96,1792]{1,0:T(8,128)(2,1)}), bf16[768,1792]{1,0:T(8,128)(2,1)}) %all-gather.8.cloned.1.call-update) | async-done | bytes 2752528 | tf_op jit(solution)/shard_map/all_gather | solution.py:51
  423.2 7.6 %fusion.2 = f32[768,1024]{1,0:T(8,128)} fusion(bf16[768,1792]{1,0:T(8,128)(2,1)} %all-gather.8.cloned.1.call-done, bf16[1792,1024]{1,0:T(8,128)(2,1)} %param.11, pred[224,8,8,128]{3,2,1,0:T(8,128)(4,1)S(1)} %bitcast.58), kind=kOutput, calls=%fused_computation.12 | convolution fusion | flops 2820407296 | bytes 11403264 | tf_op jit(solution)/shard_map/dot_general | solution.py:68
  430.8 6.3 %fusion = bf16[1024,1792]{0,1:T(8,128)(2,1)} fusion(bf16[768,1792]{1,0:T(8,128)(2,1)} %all-gather.12.cloned.1.call-done, bf16[768,1024]{1,0:T(8,128)(2,1)S(1)} %copy-done.5, pred[1024,14]{0,1:T(8,128)(4,1)S(1)} %bitcast.64), kind=kOutput, calls=%fused_computation.5 | convolution fusion | flops 2822242304 | bytes 8009728 | tf_op jit(solution)/shard_map/dot_general | solution.py:80
  437.1 6.0 %copy.37 = bf16[1024,1792]{1,0:T(8,128)(2,1)} copy(bf16[1024,1792]{0,1:T(8,128)(2,1)} %fusion) | data formatting | bytes 7340032
  443.1 6.4 %fusion.1 = bf16[1024,1792]{0,1:T(8,128)(2,1)} fusion(bf16[768,1792]{1,0:T(8,128)(2,1)} %all-gather.14.cloned.1.call-done, bf16[768,1024]{1,0:T(8,128)(2,1)S(1)} %copy-done.5, pred[1024,14]{0,1:T(8,128)(4,1)S(1)} %bitcast.62), kind=kOutput, calls=%fused_computation.6 | convolution fusion | flops 2822242304 | bytes 8009728 | tf_op jit(solution)/shard_map/dot_general | solution.py:85
  449.5 6.1 %copy.38 = bf16[1024,1792]{1,0:T(8,128)(2,1)} copy(bf16[1024,1792]{0,1:T(8,128)(2,1)} %fusion.1) | data formatting | bytes 7340032
  455.6 6.6 %select_convert_fusion = bf16[1792,1024]{1,0:T(8,128)(2,1)} fusion(pred[224,8,8,128]{3,2,1,0:T(8,128)(4,1)S(1)} %bitcast.59, bf16[768,1792]{1,0:T(8,128)(2,1)} %all-gather.8.cloned.1.call-done, bf16[768,1024]{1,0:T(8,128)(2,1)S(1)} %copy-done.4), kind=kOutput, calls=%fused_computation.7 | convolution fusion | flops 2822242304 | bytes 9830400 | tf_op jit(solution)/shard_map/dot_general | solution.py:75
  462.2 41.3 %reduce-scatter.11.cloned.1.call-done = f32[48,1024]{1,0:T(8,128)} async-done(((f32[768,1024]{1,0:T(8,128)}), f32[48,1024]{1,0:T(8,128)}) %reduce-scatter.11.cloned.1.call-update) | async-done | bytes 196624 | tf_op jit(solution)/shard_map/reduce_scatter | solution.py:89
  503.6 1.6 convert_element_type.28
  505.1 76.6 %reduce-scatter.9.cloned.1.call-done = f32[48,1024]{1,0:T(8,128)} async-done(((f32[768,1024]{1,0:T(8,128)}), f32[48,1024]{1,0:T(8,128)}) %reduce-scatter.9.cloned.1.call-update) | async-done | bytes 196624 | tf_op jit(solution)/shard_map/reduce_scatter | solution.py:67
  581.7 1.6 convert_element_type.25
  (23 shorter events, 0.2 us)
Async XLA Ops:
  7.2 53.5 %all-gather.10.cloned.1.call-start = ((), (), s32[]{:S(2)}) async-start(), calls=%async_computation.7 | async-start | bytes 1671168 | tf_op jit(solution)/shard_map/all_gather | solution.py:34
  7.9 100.7 %all-gather.6.cloned.1.call-start = ((), (), s32[]{:S(2)}) async-start(), calls=%async_computation.4 | async-start | bytes 1671168 | tf_op jit(solution)/shard_map/all_gather | solution.py:33
  8.6 166.6 %reduce-scatter.15.cloned.1.call-start = ((), (), s32[]{:S(2)}) async-start(), calls=%async_computation.12 | async-start | bytes 6193152 | tf_op jit(solution)/shard_map/reduce_scatter | solution.py:53
  80.7 0.7 copy-start.2
  80.7 0.7 copy-start.3
  80.8 213.1 %reduce-scatter.13.cloned.1.call-start = ((), (), s32[]{:S(2)}) async-start(), calls=%async_computation.11 | async-start | bytes 12386304 | tf_op jit(solution)/shard_map/reduce_scatter | solution.py:36
  94.1 4.3 copy-start
  108.6 8.1 %copy-start.1 = (bf16[1024,1792]{0,1:T(8,128)(2,1)S(1)}, bf16[1024,1792]{0,1:T(8,128)(2,1)}, u32[]{:S(2)}) copy-start(bf16[1024,1792]{0,1:T(8,128)(2,1)} %bitcast_select_fusion.3) | copy-start | bytes 11010052
  108.6 8.1 %copy-start.5 = (bf16[768,1024]{1,0:T(8,128)(2,1)S(1)}, bf16[768,1024]{1,0:T(8,128)(2,1)}, u32[]{:S(2)}) copy-start(bf16[768,1024]{1,0:T(8,128)(2,1)} %all-gather.6.cloned.1.call-done) | copy-start | bytes 4718596
  142.9 192.5 %all-gather.12.cloned.1.call-start = ((), (), s32[]{:S(2)}) async-start(), calls=%async_computation.8 | async-start | bytes 3096576 | tf_op jit(solution)/shard_map/all_gather | solution.py:64
  296.6 82.6 %all-gather.14.cloned.1.call-start = ((), (), s32[]{:S(2)}) async-start(), calls=%async_computation.9 | async-start | bytes 3096576 | tf_op jit(solution)/shard_map/all_gather | solution.py:65
  297.2 126.0 %all-gather.8.cloned.1.call-start = ((), (), s32[]{:S(2)}) async-start(), calls=%async_computation.5 | async-start | bytes 3096576 | tf_op jit(solution)/shard_map/all_gather | solution.py:51
  298.0 205.6 %reduce-scatter.11.cloned.1.call-start = ((), (), s32[]{:S(2)}) async-start(), calls=%async_computation.10 | async-start | bytes 3342336 | tf_op jit(solution)/shard_map/reduce_scatter | solution.py:89
  387.7 194.1 %reduce-scatter.9.cloned.1.call-start = ((), (), s32[]{:S(2)}) async-start(), calls=%async_computation.6 | async-start | bytes 3342336 | tf_op jit(solution)/shard_map/reduce_scatter | solution.py:67
  449.5 6.1 %copy-start.4 = (bf16[768,1024]{1,0:T(8,128)(2,1)S(1)}, bf16[768,1024]{1,0:T(8,128)(2,1)}, u32[]{:S(2)}) copy-start(bf16[768,1024]{1,0:T(8,128)(2,1)} %all-gather.10.cloned.1.call-done) | copy-start | bytes 4718596
Sparse Core Ops, SparseCore 0:
  10.4 50.2 all-gather.9
  63.1 45.4 all-gather.5
  111.1 64.1 reduce-scatter.14
  177.5 116.2 reduce-scatter.12
  296.7 38.6 all-gather.11
  336.9 42.2 all-gather.13
  380.8 42.2 all-gather.7
  427.2 76.3 reduce-scatter.10
  507.6 74.1 reduce-scatter.8
where the time goes:
time: 591 us; the launch traced here: 590 us
  waiting for transfers between devices  439 us (74%)
  matrix products  64 us (11%)
  local copies, waits for them, and re-layouts  48.8 us (8%)
  other arithmetic  23.1 us (4%)
  between operations  13.9 us (2%)
    reduce_scatter x1, waiting for transfers between devices, per_device(): lax.psum_scatter(jnp.concatenate([jnp.dot(picked, w_gate, preferred_eleme...  119 us
    reduce_scatter x1, waiting for transfers between devices, per_device(): lax.psum_scatter(jnp.dot(hidden_all, w_down, preferred_element_type=jnp.f...  76.6 us
    all_gather x1, waiting for transfers between devices, per_device(): grad_all = lax.all_gather(grad_out, 'hidden', axis=0, tiled=True)  50.9 us
    unnamed x23, local copies, waits for them, and re-layouts  43.1 us
    reduce_scatter x1, waiting for transfers between devices, per_device(): lax.psum_scatter(first + lax.dot_general(d_up_all, w_up, back, preferred_...  41.3 us
    all_gather x1, waiting for transfers between devices, per_device(): lax.all_gather(d_gate, 'width', axis=0, tiled=True)  37.2 us
    all_gather x1, waiting for transfers between devices, per_device(): lax.all_gather(d_up, 'width', axis=0, tiled=True)  36.3 us
    all_gather x1, waiting for transfers between devices, per_device(): hidden_all = lax.all_gather(hidden, 'width', axis=0, tiled=True)  35.4 us
  transfers between devices with their start and end apart: 9, of which 9 were waited for; matrix products, arithmetic and copies ran while one was open for 22% of the time, Pallas kernels for 0%

commit v1 on v0

v1 whole, which is shorter than its diff:
```python
import functools

import jax
import jax.numpy as jnp
from jax import lax
from jax.experimental import pallas as pl
from jax.experimental.pallas import tpu as pltpu
from jax.sharding import PartitionSpec as P

BLOCK = 128
COLS = 256
MESH = pl.DeviceIdType.MESH
F32 = jnp.float32
BF16 = jnp.bfloat16


def remote(src, dst, send, recv, device):
    return pltpu.make_async_remote_copy(
        src_ref=src, dst_ref=dst, send_sem=send, recv_sem=recv,
        device_id=device, device_id_type=MESH,
    )


def nt(a, b):
    return lax.dot_general(a, b, (((1,), (1,)), ((), ())), preferred_element_type=F32)


def layer_kernel(
    nk,
    tokens, gate_w, up_w, down_w, grad_out, pat_gate, pat_up, pat_down,
    output, grad_tokens, act_out, tok_out, grd_out,
    wg, wu, wd, mg, mu, md, tok, grd, own, ysend, yrecv, zsend, zrecv, ag, acc,
    csend, crecv, tsend, trecv, first,
    w_sem, o_sem, hs_sem, hr_sem, hf_sem, ys_sem, yr_sem, zs_sem, zr_sem,
    as_sem, ar_sem, cs_sem, cr_sem, ts_sem, tr_sem, act_sem, all_sem,
):
    steps = 2 * nk
    width = lax.axis_index("width")
    hid = lax.axis_index("hidden")
    z = lax.rem(width, 4)
    yl = lax.div(width, 4)
    core = lax.rem(hid, 2)
    chip = lax.div(hid, 2)
    zp, zm, zq = lax.rem(z + 1, 4), lax.rem(z + 3, 4), lax.rem(z + 2, 4)

    def at_z(to):
        return (yl * 4 + to, hid)

    partner = ((1 - yl) * 4 + z, hid)
    sibling = (width, chip * 2 + 1 - core)

    def at_chip(to, its_core):
        return (width, to * 2 + its_core)

    def place(j):
        return lax.rem(j + 4 * yl, 8)

    mine = place(chip)

    def weight_copies(k):
        cols = pl.ds(k * COLS, COLS) if isinstance(k, int) else pl.ds(pl.multiple_of(k * COLS, COLS), COLS)
        return (
            pltpu.make_async_copy(gate_w.at[:, cols], wg.at[k], w_sem.at[0, k]),
            pltpu.make_async_copy(up_w.at[:, cols], wu.at[k], w_sem.at[1, k]),
            pltpu.make_async_copy(down_w.at[cols, :], wd.at[k], w_sem.at[2, k]),
        )

    own_copies = (
        pltpu.make_async_copy(tokens, tok.at[core, mine], o_sem.at[0]),
        pltpu.make_async_copy(grad_out, grd.at[core, mine], o_sem.at[1]),
    )
    for copy in own_copies:
        copy.start()
    for k in range(nk):
        for copy in weight_copies(k):
            copy.start()

    barrier = pltpu.get_barrier_semaphore()
    for to in (zp, zm, zq):
        pl.semaphore_signal(barrier, inc=1, device_id=at_z(to), device_id_type=MESH)
    pl.semaphore_signal(barrier, inc=1, device_id=partner, device_id_type=MESH)
    pl.semaphore_signal(barrier, inc=1, device_id=sibling, device_id_type=MESH)
    for d in range(1, 8):
        for c in range(2):
            pl.semaphore_signal(
                barrier, inc=1, device_id=at_chip(lax.rem(chip + d, 8), c), device_id_type=MESH
            )
    pl.semaphore_wait(barrier, 19)

    pair = ((tokens, tok), (grad_out, grd))

    def gather_send(c):
        @pl.when(core == c)
        def _():
            for a, (src, dst) in enumerate(pair):
                def send(d, carry):
                    remote(src, dst.at[c, mine], hs_sem.at[a, d], hr_sem.at[c, a, d],
                           at_chip(lax.rem(chip + d, 8), c)).start()
                    return carry
                lax.fori_loop(1, 8, send, 0)
                remote(src, dst.at[c, mine], hs_sem.at[a, 0], hr_sem.at[c, a, 0], sibling).start()

    def arrived(c, a, d):
        dst = pair[a][1].at[c, place(lax.rem(chip + 8 - d, 8))]
        remote(dst, dst, hs_sem.at[a, d], hr_sem.at[c, a, d], sibling).wait_recv()
        return dst

    def gather_forward(c, a):
        @pl.when(core == c)
        def _():
            def hand_on(d, carry):
                dst = arrived(c, a, d)
                remote(dst, dst, hf_sem.at[a, d], hr_sem.at[c, a, d], sibling).start()
                return carry
            lax.fori_loop(1, 8, hand_on, 0)
            own_copies[a].wait()

    def gather_wait(c, a):
        @pl.when(core != c)
        def _():
            def wait(d, carry):
                arrived(c, a, d)
                return carry
            lax.fori_loop(0, 8, wait, 0)

    gather_send(0)

    blocks = COLS // BLOCK
    for b in range(nk * blocks):
        lanes = slice((b % blocks) * BLOCK, (b % blocks + 1) * BLOCK)
        for pat, mask in ((pat_gate, mg), (pat_up, mu)):
            hit = jnp.where(pat[...] == hid * (nk * blocks) + b, 1.0, 0.0)
            hit = jnp.max(hit, axis=1, keepdims=True)
            mask[b // blocks, :, lanes] = jnp.broadcast_to(hit, (8, BLOCK))
    for b in range(8):
        hit = jnp.where(pat_down[...] == width * 8 + b, 1.0, 0.0)
        hit = jnp.max(hit, axis=1, keepdims=True)
        md[:, b * BLOCK:(b + 1) * BLOCK] = jnp.broadcast_to(hit, (nk * blocks, BLOCK))

    def split(s):
        return lax.div(s, nk), lax.rem(s, nk)

    def partials(s):
        half, k = split(s)
        slot = lax.rem(s, 3)

        @pl.when(s < nk)
        def _():
            for copy in weight_copies(k):
                copy.wait()
            for r in range(8):
                rows = slice(r * BLOCK, (r + 1) * BLOCK)
                for w, mask in ((wg, mg), (wu, mu)):
                    keep = jnp.broadcast_to(mask[k, r:r + 1, :], (BLOCK, COLS)).astype(BF16)
                    w[k, rows, :] = w[k, rows, :] * keep
            for i in range(blocks):
                rows = slice(i * BLOCK, (i + 1) * BLOCK)
                row = md[pl.ds(blocks * k + i, 1), :]
                keep = jnp.broadcast_to(row, (BLOCK, row.shape[1])).astype(BF16)
                wd[k, rows, :] = wd[k, rows, :] * keep

        for c in range(2):
            @pl.when(s == c * nk)
            def _():
                if c == 0:
                    gather_forward(c, 0)
                gather_wait(c, 0)

        def put(at, value):
            cols = slice(at * COLS, (at + 1) * COLS)
            own[slot, :, :, cols] = value[:192].reshape(4, 48, COLS)
            ysend[s, :, :, cols] = value[192:].astype(BF16).reshape(4, 48, COLS)

        x = tok[half].reshape(384, -1)
        put(0, jnp.dot(x, wg[k], preferred_element_type=F32))
        put(1, jnp.dot(x, wu[k], preferred_element_type=F32))
        for c in range(2):
            @pl.when(s == c * nk)
            def _():
                if c == 0:
                    gather_forward(c, 1)
                gather_wait(c, 1)
        put(2, nt(grd[half].reshape(384, -1), wd[k]))
        remote(ysend.at[s], yrecv.at[s], ys_sem.at[s], yr_sem.at[s], partner).start()

        @pl.when(s == 0)
        def _():
            gather_send(1)

        @pl.when(s == nk - 2)
        def _():
            gather_forward(1, 0)
            gather_forward(1, 1)

    def pair_sum(s, at):
        return own[lax.rem(s, 3), at] + yrecv[s, at].astype(F32)

    def after_pair(s):
        remote(ysend.at[s], yrecv.at[s], ys_sem.at[s], yr_sem.at[s], partner).wait_recv()
        for i, to in enumerate((zp, zm, zq)):
            zsend[s, i] = pair_sum(s, to).astype(BF16)
            remote(zsend.at[s, i], zrecv.at[s, i], zs_sem.at[s, i], zr_sem.at[s, i], at_z(to)).start()

    def ag_copy(s, i):
        src, to = (
            ((0, z), at_z(zp)), ((0, z), at_z(zm)), ((0, z), partner),
            ((1, z), at_z(zp)), ((1, z), at_z(zm)),
            ((0, zp), at_z(zm)), ((1, zm), at_z(zp)),
        )[i]
        here = ag.at[s, src[0], src[1]]
        there = ag.at[s, 1, z] if i == 2 else here
        return remote(here, there, as_sem.at[s, i], ar_sem.at[s, i], to)

    def ag_wait(s, i):
        y, at = ((0, zm), (0, zp), (1, z), (1, zm), (1, zp), (0, zq), (1, zq))[i]
        here = ag.at[s, y, at]
        remote(here, here, as_sem.at[s, i], ar_sem.at[s, i], partner).wait_recv()

    def activate(s):
        for i in range(3):
            remote(zsend.at[s, i], zrecv.at[s, i], zs_sem.at[s, i], zr_sem.at[s, i], at_z(zp)).wait_recv()
        total = pair_sum(s, z)
        for i in range(3):
            total = total + zrecv[s, i].astype(F32)
        gate, up, gh = total[:, :COLS], total[:, COLS:2 * COLS], total[:, 2 * COLS:]
        sig = 1.0 / (1.0 + jnp.exp(-gate))
        silu = gate * sig
        ag[s, 0, z, :, :COLS] = (silu * up).astype(BF16)
        ag[s, 0, z, :, COLS:2 * COLS] = (gh * up * sig * (1.0 + gate * (1.0 - sig))).astype(BF16)
        ag[s, 0, z, :, 2 * COLS:] = (gh * silu).astype(BF16)
        for i in (2, 0, 1):
            ag_copy(s, i).start()

    def pass_partner(s):
        ag_wait(s, 2)
        ag_copy(s, 3).start()
        ag_copy(s, 4).start()

    def pass_on(s):
        ag_wait(s, 1)
        ag_copy(s, 5).start()
        ag_wait(s, 3)
        ag_copy(s, 6).start()

    def back(s):
        half, k = split(s)
        for i in (0, 4, 5, 6):
            ag_wait(s, i)
        pltpu.make_async_copy(ag.at[s], act_out.at[s], act_sem.at[s]).start()

        @pl.when(k == 0)
        def _():
            acc[half] = jnp.zeros(acc.shape[1:], F32)

        hidden = ag[s, :, :, :, :COLS].reshape(384, COLS)
        d_gate = ag[s, :, :, :, COLS:2 * COLS].reshape(384, COLS)
        d_up = ag[s, :, :, :, 2 * COLS:].reshape(384, COLS)
        for n in range(4):
            cols = slice(n * 256, (n + 1) * 256)
            acc[half, 0, :, cols] += jnp.dot(hidden, wd[k, :, cols], preferred_element_type=F32)
            acc[half, 1, :, cols] += nt(d_gate, wg[k, cols, :]) + nt(d_up, wu[k, cols, :])

    def rows48(p):
        return pl.ds(pl.multiple_of(p * 48, 48), 48)

    def tail_pair(half):
        def send(d, carry):
            p = place(lax.rem(chip + d, 8))
            csend[half, p] = acc[half, 1 - core, rows48(p), :].astype(BF16)
            remote(csend.at[half, p], crecv.at[half, p], cs_sem.at[half, d], cr_sem.at[half, d], sibling).start()
            return carry
        lax.fori_loop(0, 8, send, 0)

    def tail_send(half):
        def send(d, carry):
            p = place(lax.rem(chip + d, 8))
            remote(csend.at[half, p], crecv.at[half, p], cs_sem.at[half, d], cr_sem.at[half, d], sibling).wait_recv()
            total = acc[half, core, rows48(p), :] + crecv[half, p].astype(F32)

            @pl.when(d > 0)
            def _():
                tsend[half, p] = total.astype(BF16)
                remote(tsend.at[half, p], trecv.at[core, d], ts_sem.at[half, d], tr_sem.at[core, d],
                       at_chip(lax.rem(chip + d, 8), half)).start()

            @pl.when((d == 0) & (core == half))
            def _():
                first[core] = total

            @pl.when((d == 0) & (core != half))
            def _():
                tsend[half, p] = total.astype(BF16)
                remote(tsend.at[half, p], trecv.at[core, 0], ts_sem.at[half, 0], tr_sem.at[core, 0], sibling).start()
            return carry
        lax.fori_loop(0, 8, send, 0)

    def tail_sum(half):
        @pl.when(core == half)
        def _():
            def landed(a, d):
                remote(trecv.at[a, d], trecv.at[a, d], ts_sem.at[half, d], tr_sem.at[a, d], sibling).wait_recv()
            landed(1 - half, 0)
            first[1 - half] = trecv[1 - half, 0].astype(F32)
            for a, out in enumerate((output, grad_tokens)):
                total = first[a]
                for d in range(1, 8):
                    landed(a, d)
                    total = total + trecv[a, d].astype(F32)
                out[...] = total.astype(BF16)

    last = steps + 5

    def step(t, carry):
        def run(offset, what):
            s = t - offset

            @pl.when((s >= 0) & (s < steps))
            def _():
                what(s)

        run(0, partials)
        run(1, after_pair)
        run(2, activate)
        run(3, pass_partner)
        run(4, pass_on)
        run(5, back)

        @pl.when(t == nk + 5)
        def _():
            tail_pair(0)
            pltpu.make_async_copy(tok, tok_out, all_sem.at[0]).start()
            pltpu.make_async_copy(grd, grd_out, all_sem.at[1]).start()

        @pl.when(t == nk + 6)
        def _():
            tail_send(0)
        return carry

    lax.fori_loop(0, last, step, 0)
    tail_pair(1)
    tail_send(1)
    tail_sum(0)
    tail_sum(1)

    def drain(s, carry):
        remote(ysend.at[s], yrecv.at[s], ys_sem.at[s], yr_sem.at[s], partner).wait_send()
        for i in range(3):
            remote(zsend.at[s, i], zrecv.at[s, i], zs_sem.at[s, i], zr_sem.at[s, i], partner).wait_send()
        for i in range(7):
            ag_copy(s, i).wait_send()
        pltpu.make_async_copy(ag.at[s], act_out.at[s], act_sem.at[s]).wait()
        return carry

    lax.fori_loop(0, steps, drain, 0)
    for a, (src, dst) in enumerate(pair):
        remote(src, dst.at[core, mine], hs_sem.at[a, 0], hr_sem.at[0, a, 0], sibling).wait_send()

        def gone(d, carry):
            remote(src, dst.at[core, mine], hs_sem.at[a, d], hr_sem.at[0, a, d], sibling).wait_send()
            there = dst.at[core, place(lax.rem(chip + 8 - d, 8))]
            remote(there, there, hf_sem.at[a, d], hr_sem.at[0, a, d], sibling).wait_send()
            return carry
        lax.fori_loop(1, 8, gone, 0)
    for half in range(2):
        def sent(d, carry):
            p = place(lax.rem(chip + d, 8))
            remote(csend.at[half, p], crecv.at[half, p], cs_sem.at[half, d], cr_sem.at[half, d], sibling).wait_send()

            @pl.when((d > 0) | (core != half))
            def _():
                remote(tsend.at[half, p], trecv.at[core, d], ts_sem.at[half, d], tr_sem.at[core, d], sibling).wait_send()
            return carry
        lax.fori_loop(0, 8, sent, 0)
    pltpu.make_async_copy(tok, tok_out, all_sem.at[0]).wait()
    pltpu.make_async_copy(grd, grd_out, all_sem.at[1]).wait()


def layer(tokens, gate_w, up_w, down_w, grad_out, pat_gate, pat_up, pat_down):
    rows, width = tokens.shape
    hidden = gate_w.shape[1]
    nk = hidden // COLS
    steps = 2 * nk
    any_, vmem = pl.BlockSpec(memory_space=pl.ANY), pl.BlockSpec(memory_space=pltpu.VMEM)
    dma, three = pltpu.SemaphoreType.DMA, 3 * COLS
    small = jax.ShapeDtypeStruct((rows, width), BF16)
    gathered = jax.ShapeDtypeStruct((2, 8, rows, width), BF16)
    return pl.pallas_call(
        functools.partial(layer_kernel, nk),
        name="layer",
        out_shape=(small, small, jax.ShapeDtypeStruct((steps, 2, 4, rows, three), BF16), gathered, gathered),
        in_specs=[any_] * 5 + [vmem] * 3,
        out_specs=(vmem, vmem, any_, any_, any_),
        scratch_shapes=[
            pltpu.VMEM((nk, width, COLS), BF16),
            pltpu.VMEM((nk, width, COLS), BF16),
            pltpu.VMEM((nk, COLS, width), BF16),
            pltpu.VMEM((nk, 8, COLS), F32),
            pltpu.VMEM((nk, 8, COLS), F32),
            pltpu.VMEM((hidden // BLOCK, width), F32),
            pltpu.VMEM((2, 8, rows, width), BF16),
            pltpu.VMEM((2, 8, rows, width), BF16),
            pltpu.VMEM((3, 4, rows, three), F32),
            pltpu.VMEM((steps, 4, rows, three), BF16),
            pltpu.VMEM((steps, 4, rows, three), BF16),
            pltpu.VMEM((steps, 3, rows, three), BF16),
            pltpu.VMEM((steps, 3, rows, three), BF16),
            pltpu.VMEM((steps, 2, 4, rows, three), BF16),
            pltpu.VMEM((2, 2, 8 * rows, width), F32),
            pltpu.VMEM((2, 8, rows, width), BF16),
            pltpu.VMEM((2, 8, rows, width), BF16),
            pltpu.VMEM((2, 8, rows, width), BF16),
            pltpu.VMEM((2, 8, rows, width), BF16),
            pltpu.VMEM((2, rows, width), F32),
            dma((3, nk)), dma((2,)), dma((2, 8)), dma((2, 2, 8)), dma((2, 8)),
            dma((steps,)), dma((steps,)), dma((steps, 3)), dma((steps, 3)),
            dma((steps, 7)), dma((steps, 7)), dma((2, 8)), dma((2, 8)),
            dma((2, 8)), dma((2, 8)), dma((steps,)), dma((2,)),
        ],
        compiler_params=pltpu.CompilerParams(
            collective_id=0, has_side_effects=True, vmem_limit_bytes=60 * 2**20
        ),
    )(tokens, gate_w, up_w, down_w, grad_out, pat_gate, pat_up, pat_down)


def weight_grads_kernel(act, tok, grd, pat_gate, pat_up, pat_down, grad_gate, grad_up, grad_down):
    k = pl.program_id(0)
    hid = lax.axis_index("hidden")
    width = lax.axis_index("width")
    blocks = COLS // BLOCK
    per = pl.num_programs(0) * blocks
    contract = (((0,), (0,)), ((), ()))
    rows = tok.shape[0]
    x = tok[...]
    for at, pat, out in ((1, pat_gate, grad_gate), (2, pat_up, grad_up)):
        d = act[:, 0, :, at * COLS:(at + 1) * COLS].reshape(rows, COLS)
        res = lax.dot_general(x, d, contract, preferred_element_type=F32)
        for b in range(blocks):
            hit = jnp.where(pat[...] == hid * per + k * blocks + b, 1.0, 0.0)
            hit = jnp.max(hit, axis=1, keepdims=True)
            lanes = slice(b * BLOCK, (b + 1) * BLOCK)
            for r in range(8):
                rs = slice(r * BLOCK, (r + 1) * BLOCK)
                keep = jnp.broadcast_to(hit[r:r + 1, :], (BLOCK, BLOCK))
                out[rs, lanes] = jnp.where(keep > 0.0, res[rs, lanes], 0.0).astype(BF16)
    h = act[:, 0, :, :COLS].reshape(rows, COLS)
    res = lax.dot_general(h, grd[...], contract, preferred_element_type=F32)
    for i in range(blocks):
        row = pat_down[pl.ds(k * blocks + i, 1), :]
        rs = slice(i * BLOCK, (i + 1) * BLOCK)
        for b in range(8):
            hit = jnp.max(jnp.where(row == width * 8 + b, 1.0, 0.0), axis=1, keepdims=True)
            lanes = slice(b * BLOCK, (b + 1) * BLOCK)
            keep = jnp.broadcast_to(hit, (BLOCK, BLOCK))
            grad_down[rs, lanes] = jnp.where(keep > 0.0, res[rs, lanes], 0.0).astype(BF16)


def weight_grads(act, tok, grd, pat_gate, pat_up, pat_down):
    nk = act.shape[0] // 2
    tokens, width = 2 * act.shape[1], tok.shape[1]
    hidden = nk * COLS
    whole = lambda k: (0, 0)
    return pl.pallas_call(
        weight_grads_kernel,
        name="weight_grads",
        grid=(nk,),
        out_shape=(
            jax.ShapeDtypeStruct((width, hidden), BF16),
            jax.ShapeDtypeStruct((width, hidden), BF16),
            jax.ShapeDtypeStruct((hidden, width), BF16),
        ),
        in_specs=[
            pl.BlockSpec((2, 1, tokens // 2, 3 * COLS), lambda k: (0, k, 0, 0)),
            pl.BlockSpec((tokens, width), whole),
            pl.BlockSpec((tokens, width), whole),
            pl.BlockSpec(pat_gate.shape, whole),
            pl.BlockSpec(pat_up.shape, whole),
            pl.BlockSpec(pat_down.shape, whole),
        ],
        out_specs=(
            pl.BlockSpec((width, COLS), lambda k: (0, k)),
            pl.BlockSpec((width, COLS), lambda k: (0, k)),
            pl.BlockSpec((COLS, width), lambda k: (k, 0)),
        ),
        compiler_params=pltpu.CompilerParams(vmem_limit_bytes=48 * 2**20),
    )(act.reshape(2, nk, tokens // 2, 3 * COLS), tok, grd, pat_gate, pat_up, pat_down)


def per_device(
    tokens, gate_weight, up_weight, down_weight, grad_out, pattern_gate, pattern_up, pattern_down
):
    output, grad_tokens, act, tok, grd = layer(
        tokens, gate_weight, up_weight, down_weight, grad_out, pattern_gate, pattern_up, pattern_down
    )
    rows, width = tokens.shape
    grad_gate, grad_up, grad_down = weight_grads(
        act.reshape(act.shape[0], 8 * rows, 3 * COLS),
        tok.reshape(16 * rows, width),
        grd.reshape(16 * rows, width),
        pattern_gate, pattern_up, pattern_down,
    )
    return output, grad_tokens, grad_gate, grad_up, grad_down


def solution(mesh):
    placed = (
        P("hidden", "width"),
        P("width", "hidden"),
        P("width", "hidden"),
        P("hidden", "width"),
        P("hidden", "width"),
        P("width", None),
        P("width", None),
        P("hidden", None),
    )
    return jax.shard_map(
        per_device,
        mesh=mesh,
        in_specs=placed,
        out_specs=(
            P("hidden", "width"),
            P("hidden", "width"),
            P("width", "hidden"),
            P("width", "hidden"),
            P("hidden", "width"),
        ),
        check_vma=False,
    )
```

time: 591 us -> 202 us (0.34)
  waiting for transfers between devices: 439 us -> 0 us
  Pallas kernels: 0 us -> 197 us
  matrix products: 64 us -> 0 us
  local copies, waits for them, and re-layouts: 48.8 us -> 4.11 us
  other arithmetic: 23.1 us -> 0 us
  between operations: 13.9 us -> 0.7 us
    reduce_scatter x4 -> x0, waiting for transfers between devices: 269 us -> none  [the longest x1 119 us: per_device(): lax.psum_scatter(jnp.concatenate([jnp.dot(picked, w_gate, preferred_eleme...]
    pallas_call x0 -> x2, Pallas kernels: none -> 197 us  [the longest x1 184 us: layer(): pl.pallas_call(functools.partial(layer_kernel, nk), name='layer', out_sha...]
    all_gather x5 -> x0, waiting for transfers between devices: 168 us -> none  [the longest x1 50.9 us: per_device(): grad_all = lax.all_gather(grad_out, 'hidden', axis=0, tiled=True)]
    dot_general x9 -> x0, matrix products: 64 us -> none  [the longest x1 8.44 us: per_device(): lax.dot_general(d_up_all, w_up, back, preferred_element_type=jnp.float32)]
    unnamed x23 -> x16, local copies, waits for them, and re-layouts: 43.1 us -> 4.11 us
    concatenate x1 -> x0, other arithmetic: 9.08 us -> none  [per_device(): jnp.concatenate([jnp.dot(picked, w_gate, preferred_element_type=jnp.float...]
    select_n x2 -> x0, other arithmetic: 6.41 us -> none  [the longest x1 4.3 us: per_device(): w_up = jnp.where(mask_up, up_weight, zero)]
    convert_element_type x3 -> x0, other arithmetic: 5.92 us -> none  [the longest x1 2.77 us: per_device(): d_up = (grad_hidden * gate * sig).astype(jnp.bfloat16)]
  transfers between devices with their start and end apart: 9 -> 0, of which waited for: 9 -> 0; matrix products, arithmetic and copies ran while one was open for 22% -> 0% of each run, Pallas kernels for 0% -> 0%
where the time goes in v1:
time: 202 us
  Pallas kernels  197 us (98%)
  local copies, waits for them, and re-layouts  4.11 us (2%)
    pallas_call x1, Pallas kernels, layer(): pl.pallas_call(functools.partial(layer_kernel, nk), name='layer', out_sha...  184 us
    pallas_call x1, Pallas kernels, weight_grads(): pl.pallas_call(weight_grads_kernel, name='weight_grads', grid=(nk,), out_...  12.9 us
    unnamed x16, local copies, waits for them, and re-layouts  4.11 us

profile of v1, /device:TPU:1, one launch (start us, length us, event | category | flops | bytes accessed | tf_op | source)
XLA Modules:
  0.0 202.0 jit_solution(2994859990821380925)
XLA Ops:
  0.6 0.0 copy-start.2
  0.6 0.0 copy-start.4
  0.7 0.0 copy-start.3
  0.7 184.3 %layer.1 = (bf16[48,1024]{1,0:T(8,128)(2,1)}, bf16[48,1024]{1,0:T(8,128)(2,1)}, bf16[14,2,4,48,768]{4,3,2,1,0:T(8,128)(2,1)}, bf16[2,8,48,1024]{3,2,1,0:T(8,128)(2,1)}, bf16[2,8,48,1024]{3,2,1,0:T(8,128)(2,1)}) custom-call(bf16[48,1024]{1,0:T(8,128)(2,1)} %tokens.1, bf16[1024,1792]{1,0:T(8,128)(2,1)} %gate_w.1, bf16[1024,1792]{1,0:T(8,128)(2,1)} %up_w.1, ...), custom_call_target="tpu_custom_call" | custom-call | tf_op jit(solution)/shard_map/layer/pallas_call | solution.py:387
  184.9 0.0 copy-done.2
  184.9 0.0 copy-done.4
  185.0 0.0 copy-done.3
  185.0 0.0 copy-start
  185.0 1.4 copy-done
  186.4 0.0 copy-start.1
  186.4 1.4 copy-done.1
  187.8 0.0 copy-start.6
  187.8 0.0 copy-start.5
  187.8 12.9 %weight_grads.1 = (bf16[1024,1792]{1,0:T(8,128)(2,1)}, bf16[1024,1792]{1,0:T(8,128)(2,1)}, bf16[1792,1024]{1,0:T(8,128)(2,1)}) custom-call(bf16[2,7,384,768]{3,2,1,0:T(8,128)(2,1)} %bitcast.5, bf16[768,1024]{1,0:T(8,128)(2,1)S(1)} %bitcast.3, bf16[768,1024]{1,0:T(8,128)(2,1)S(1)} %bitcast.4, s32[8,112]{1,0:T(8,128)S(1)} %copy-done.3, ...), custom_call_target="tpu_custom_call" | custom-call | tf_op jit(solution)/shard_map/weight_grads/pallas_call | solution.py:462
  200.7 0.0 copy-done.6
  200.7 0.6 copy.15
  201.3 0.0 copy-done.5
  201.3 0.6 copy.16
Async XLA Ops:
  0.6 184.3 %copy-start.2 = (s32[14,32]{1,0:T(8,128)S(1)}, s32[14,32]{1,0:T(8,128)}, u32[]{:S(2)}) copy-start(s32[14,32]{1,0:T(8,128)} %pat_down.3) | copy-start | bytes 5380
  0.6 184.3 %copy-start.4 = (s32[8,112]{1,0:T(8,128)S(1)}, s32[8,112]{1,0:T(8,128)}, u32[]{:S(2)}) copy-start(s32[8,112]{1,0:T(8,128)} %pat_up.3) | copy-start | bytes 10756
  0.7 184.3 %copy-start.3 = (s32[8,112]{1,0:T(8,128)S(1)}, s32[8,112]{1,0:T(8,128)}, u32[]{:S(2)}) copy-start(s32[8,112]{1,0:T(8,128)} %pat_gate.3) | copy-start | bytes 10756
  185.0 1.4 copy-start
  186.4 1.4 copy-start.1
  187.8 12.9 %copy-start.6 = (bf16[48,1024]{1,0:T(8,128)(2,1)S(1)}, bf16[48,1024]{1,0:T(8,128)(2,1)}, u32[]{:S(2)}) copy-start(bf16[48,1024]{1,0:T(8,128)(2,1)} %get-tuple-element.26) | copy-start | bytes 294916
  187.8 13.5 %copy-start.5 = (bf16[48,1024]{1,0:T(8,128)(2,1)S(1)}, bf16[48,1024]{1,0:T(8,128)(2,1)}, u32[]{:S(2)}) copy-start(bf16[48,1024]{1,0:T(8,128)(2,1)} %get-tuple-element.27) | copy-start | bytes 294916

commit v2 on v0

v2 whole, which is shorter than its diff:
```python
import functools

import jax
import jax.numpy as jnp
from jax import lax
from jax.experimental import pallas as pl
from jax.experimental.pallas import tpu as pltpu
from jax.sharding import PartitionSpec as P

BLOCK = 128
COLS = 256
PARTS = 3
PIECE = 16
LAGS = (0, 1, 2, 3, 4, 5)
SLOTS = 4
DIRECT = 1
CUTS = 8
MESH = pl.DeviceIdType.MESH
F32 = jnp.float32
BF16 = jnp.bfloat16


def remote(src, dst, send, recv, device):
    return pltpu.make_async_remote_copy(
        src_ref=src, dst_ref=dst, send_sem=send, recv_sem=recv,
        device_id=device, device_id_type=MESH,
    )


def nt(a, b):
    return lax.dot_general(a, b, (((1,), (1,)), ((), ())), preferred_element_type=F32)


def layer_kernel(
    nk,
    tokens, gate_w, up_w, down_w, grad_out, pat_gate, pat_up, pat_down,
    output, grad_tokens, grad_gate, grad_up, grad_down,
    wg, wu, wd, mg, mu, md, tok, grd, own, ysend, yrecv, zsend, zrecv, ag, acc,
    crecv, xsend, xrecv, kept, fsend, frecv, gg, gu, gd, lsend, lrecv,
    w_sem, o_sem, hs_sem, hr_sem, ys_sem, yr_sem, zs_sem, zr_sem,
    as_sem, ar_sem, cs_sem, cr_sem, xs_sem, xr_sem, fs_sem, fr_sem, g_sem, ls_sem, lr_sem, y0_sem,
):
    steps = PARTS * nk
    width = lax.axis_index("width")
    hid = lax.axis_index("hidden")
    z = lax.rem(width, 4)
    yl = lax.div(width, 4)
    core = lax.rem(hid, 2)
    yh = lax.rem(lax.div(hid, 2), 2)
    x = lax.div(hid, 4)
    zp, zm, zq = lax.rem(z + 1, 4), lax.rem(z + 3, 4), lax.rem(z + 2, 4)
    xp, xm, xq = lax.rem(x + 1, 4), lax.rem(x + 3, 4), lax.rem(x + 2, 4)

    def at_z(to):
        return (yl * 4 + to, hid)

    def other_y(to):
        return ((1 - yl) * 4 + to, hid)

    def at_chip(its_x, its_yh):
        return (width, its_x * 4 + its_yh * 2 + core)

    def at_x(to):
        return at_chip(to, yh)

    partner = ((1 - yl) * 4 + z, hid)
    sibling = (width, hid + 1 - 2 * core)
    across = (width, x * 4 + (1 - yh) * 2 + core)

    def place(its_x, its_yh):
        return lax.rem(its_x * 2 + its_yh + 4 * yl, 8)

    def weight_copies(k):
        cols = pl.ds(k * COLS, COLS) if isinstance(k, int) else pl.ds(pl.multiple_of(k * COLS, COLS), COLS)
        return (
            pltpu.make_async_copy(gate_w.at[:, cols], wg.at[k], w_sem.at[0, k]),
            pltpu.make_async_copy(up_w.at[:, cols], wu.at[k], w_sem.at[1, k]),
            pltpu.make_async_copy(down_w.at[cols, :], wd.at[k], w_sem.at[2, k]),
        )

    pair = ((tokens, tok), (grad_out, grd))

    def own_copy(p, a):
        src, dst = pair[a]
        return pltpu.make_async_copy(
            src.at[pl.ds(p * PIECE, PIECE)], dst.at[p, place(x, yh), core], o_sem.at[a, p]
        )

    for p in range(PARTS):
        for a in range(2):
            own_copy(p, a).start()
    for copy in weight_copies(0):
        copy.start()

    barrier = pltpu.get_barrier_semaphore()
    friends = [at_z(zp), at_z(zm), at_z(zq), partner, other_y(zp), other_y(zm), other_y(zq), sibling, across]
    friends += [at_chip(to, its_yh) for to in (xp, xm, xq) for its_yh in (yh, 1 - yh)]
    for friend in friends:
        pl.semaphore_signal(barrier, inc=1, device_id=friend, device_id_type=MESH)
    pl.semaphore_wait(barrier, len(friends))

    def gathered(p, a, i):
        its_x = (x, x, xm, xp, xq, xm, xp, xq)[i if i < 8 else i - 7]
        its_yh = (yh, 1 - yh, yh, yh, yh, 1 - yh, 1 - yh, 1 - yh)[i if i < 8 else i - 7]
        its_core = core if 0 < i < 8 else 1 - core
        return pair[a][1].at[p, place(its_x, its_yh), its_core]

    def gather_copy(p, a, i):
        to = (sibling, across, at_x(xp), at_x(xm), at_x(xq), at_x(xp), at_x(xm), at_x(xq))
        if i < 5:
            src = dst = pair[a][1].at[p, place(x, yh), core]
        elif i < 8 and p == 0:
            src = dst = pair[a][1].at[p, place(x, yh), core]
        elif i < 8:
            src = dst = gathered(p, a, 1)
        else:
            src = dst = gathered(p, a, i - 7)
        if p == 0:
            to = to[:5] + (at_chip(xp, 1 - yh), at_chip(xm, 1 - yh), at_chip(xq, 1 - yh))
        return remote(src, dst, hs_sem.at[p, a, i], hr_sem.at[p, a, i], to[i] if i < 8 else sibling)

    def gather_arrived(p, a, i):
        dst = gathered(p, a, i)
        remote(dst, dst, hs_sem.at[p, a, i], hr_sem.at[p, a, i], sibling).wait_recv()

    def gather_send(p, a):
        own_copy(p, a).wait()
        for i in (1, 5, 6, 7, 2, 3, 4, 0) if p == 0 else (1, 2, 3, 4, 0):
            gather_copy(p, a, i).start()

    def gather_across(p, a):
        gather_arrived(p, a, 1)
        for i in (8,) if p == 0 else (5, 6, 7, 8):
            gather_copy(p, a, i).start()

    def gather_share(p, a):
        for i in range(2, 8):
            gather_arrived(p, a, i)
            gather_copy(p, a, i + 7).start()

    def gather_wait(p, a):
        for i in (0, *range(8, 15)):
            gather_arrived(p, a, i)

    for a in range(2):
        gather_send(0, a)
    for k in range(1, nk):
        for copy in weight_copies(k):
            copy.start()

    blocks = COLS // BLOCK
    for b in range(nk * blocks):
        lanes = slice((b % blocks) * BLOCK, (b % blocks + 1) * BLOCK)
        for pat, mask in ((pat_gate, mg), (pat_up, mu)):
            hit = jnp.where(pat[...] == hid * (nk * blocks) + b, 1.0, 0.0)
            hit = jnp.max(hit, axis=1, keepdims=True)
            mask[b // blocks, :, lanes] = jnp.broadcast_to(hit, (8, BLOCK))
    for b in range(8):
        hit = jnp.where(pat_down[...] == width * 8 + b, 1.0, 0.0)
        hit = jnp.max(hit, axis=1, keepdims=True)
        md[:, b * BLOCK:(b + 1) * BLOCK] = jnp.broadcast_to(hit, (nk * blocks, BLOCK))

    def split(s):
        return lax.div(s, nk), lax.rem(s, nk)

    rows = 16 * PIECE
    half, slot_rows = rows // 2, rows // 8

    def masked_weights(k):
        for copy in weight_copies(k):
            copy.wait()
        for r in range(8):
            at = slice(r * BLOCK, (r + 1) * BLOCK)
            for w, mask in ((wg, mg), (wu, mu)):
                keep = jnp.broadcast_to(mask[k, r:r + 1, :], (BLOCK, COLS)).astype(BF16)
                w[k, at, :] = w[k, at, :] * keep
        for i in range(blocks):
            at = slice(i * BLOCK, (i + 1) * BLOCK)
            row = md[pl.ds(blocks * k + i, 1), :]
            keep = jnp.broadcast_to(row, (BLOCK, row.shape[1])).astype(BF16)
            wd[k, at, :] = wd[k, at, :] * keep

    def first_copy(i):
        cols = (pl.ds(0, 2 * COLS), pl.ds(2 * COLS, COLS))[i]
        return remote(ysend.at[0, :, :, cols], yrecv.at[0, :, :, cols], y0_sem.at[i], y0_sem.at[2 + i], partner)

    def partials(s):
        part, k = split(s)
        slot = lax.rem(s, SLOTS)

        @pl.when(s < nk)
        def _():
            masked_weights(k)

        for p in range(1, PARTS):
            @pl.when(s == p * nk)
            def _():
                gather_wait(p, 0)
                gather_wait(p, 1)

        @pl.when(s == 0)
        def _():
            gather_across(0, 0)
            gather_share(0, 0)
            gather_wait(0, 0)

        def put(at, value):
            cols = slice(at * COLS, (at + 1) * COLS)
            own[slot, :, :, cols] = value[:half].reshape(4, slot_rows, COLS)
            ysend[s, :, :, cols] = value[half:].astype(BF16).reshape(4, slot_rows, COLS)

        t = tok[part].reshape(rows, -1)
        put(0, jnp.dot(t, wg[k], preferred_element_type=F32))
        put(1, jnp.dot(t, wu[k], preferred_element_type=F32))

        @pl.when(s == 0)
        def _():
            first_copy(0).start()
            gather_across(0, 1)
            gather_share(0, 1)
            gather_wait(0, 1)
        put(2, nt(grd[part].reshape(rows, -1), wd[k]))

        @pl.when(s == 0)
        def _():
            first_copy(1).start()

        @pl.when(s > 0)
        def _():
            remote(ysend.at[s], yrecv.at[s], ys_sem.at[s], yr_sem.at[s], partner).start()

        for p in range(1, PARTS):
            for at, what in ((0, gather_send), (2, gather_across), (4, gather_share)):
                @pl.when(s == (p - 1) * nk + at)
                def _():
                    what(p, 0)
                    what(p, 1)

    def pair_sum(s, at):
        return own[lax.rem(s, SLOTS), at] + yrecv[s, at].astype(F32)

    def after_pair(s):
        @pl.when(s == 0)
        def _():
            for i in range(2):
                first_copy(i).wait_recv()

        @pl.when(s > 0)
        def _():
            remote(ysend.at[s], yrecv.at[s], ys_sem.at[s], yr_sem.at[s], partner).wait_recv()
        for i, to in enumerate((zp, zm, zq)):
            zsend[s, i] = pair_sum(s, to).astype(BF16)
            remote(zsend.at[s, i], zrecv.at[s, i], zs_sem.at[s, i], zr_sem.at[s, i], at_z(to)).start()

    def ag_copy(s, i):
        src, to = (
            ((0, z), at_z(zp)), ((0, z), at_z(zm)), ((0, z), partner),
            ((1, z), at_z(zp)), ((1, z), at_z(zm)),
            ((0, zp), at_z(zm)), ((1, zm), at_z(zp)),
        )[i]
        here = ag.at[s, src[0], src[1]]
        there = ag.at[s, 1, z] if i == 2 else here
        return remote(here, there, as_sem.at[s, i], ar_sem.at[s, i], to)

    def ag_direct(s, i):
        to = (other_y(zp), other_y(zm), at_z(zq), other_y(zq))[i - 3]
        there = ag.at[s, 0 if i == 5 else 1, z]
        return remote(ag.at[s, 0, z], there, as_sem.at[s, i], ar_sem.at[s, i], to)

    def ag_wait(s, i):
        y, at = ((0, zm), (0, zp), (1, z), (1, zm), (1, zp), (0, zq), (1, zq))[i]
        here = ag.at[s, y, at]
        remote(here, here, as_sem.at[s, i], ar_sem.at[s, i], partner).wait_recv()

    def activate(s):
        for i in range(3):
            remote(zsend.at[s, i], zrecv.at[s, i], zs_sem.at[s, i], zr_sem.at[s, i], at_z(zp)).wait_recv()
        total = pair_sum(s, z)
        for i in range(3):
            total = total + zrecv[s, i].astype(F32)
        gate, up, gh = total[:, :COLS], total[:, COLS:2 * COLS], total[:, 2 * COLS:]
        sig = 1.0 / (1.0 + jnp.exp(-gate))
        silu = gate * sig
        ag[s, 0, z, :, :COLS] = (silu * up).astype(BF16)
        ag[s, 0, z, :, COLS:2 * COLS] = (gh * up * sig * (1.0 + gate * (1.0 - sig))).astype(BF16)
        ag[s, 0, z, :, 2 * COLS:] = (gh * silu).astype(BF16)
        for i in (2, 0, 1):
            ag_copy(s, i).start()

        @pl.when(s >= steps - DIRECT)
        def _():
            for i in (3, 4, 5, 6):
                ag_direct(s, i).start()

    def pass_partner(s):
        ag_wait(s, 2)

        @pl.when(s < steps - DIRECT)
        def _():
            ag_copy(s, 3).start()
            ag_copy(s, 4).start()

    def pass_on(s):
        ag_wait(s, 1)

        @pl.when(s < steps - DIRECT)
        def _():
            ag_copy(s, 5).start()
        ag_wait(s, 3)

        @pl.when(s < steps - DIRECT)
        def _():
            ag_copy(s, 6).start()

    def back(s):
        part, k = split(s)
        slot = lax.rem(part, 2)
        for i in (0, 4, 5, 6):
            ag_wait(s, i)

        @pl.when(s == 2 * nk)
        def _():
            for i in range(8):
                tail_copy(0, i).wait_send()

        @pl.when(k == 0)
        def _():
            acc[slot] = jnp.zeros(acc.shape[1:], F32)

        hidden = ag[s, :, :, :, :COLS].reshape(rows, COLS)
        d_gate = ag[s, :, :, :, COLS:2 * COLS].reshape(rows, COLS)
        d_up = ag[s, :, :, :, 2 * COLS:].reshape(rows, COLS)
        for n in range(4):
            cols = slice(n * 256, (n + 1) * 256)
            acc[slot, 0, :, cols] += jnp.dot(hidden, wd[k, :, cols], preferred_element_type=F32)
            acc[slot, 1, :, cols] += nt(d_gate, wg[k, cols, :]) + nt(d_up, wu[k, cols, :])

    def tail_chip(i):
        return (xp, xm, xq, x)[i // 2], i % 2

    def tail_rows(i, its_core):
        return pl.ds(pl.multiple_of(place(*tail_chip(i)) * slot_rows + its_core * PIECE, PIECE), PIECE)

    def tail_copy(p, i):
        return remote(
            acc.at[p % 2, :, tail_rows(i, 1 - core), :], crecv.at[p, i], cs_sem.at[p, i], cr_sem.at[p, i], sibling
        )

    def tail_pair(p):
        for i in range(8):
            tail_copy(p, i).start()

    def core_sum(p, i):
        return acc[p % 2, :, tail_rows(i, core), :] + crecv[p, i]

    def x_copy(p, i):
        return remote(xsend.at[p, i], xrecv.at[p, i], xs_sem.at[p, i], xr_sem.at[p, i], at_x((xp, xm, xq)[i]))

    def tail_x(p):
        for i in range(8):
            tail_copy(p, i).wait_recv()
            if i < 6:
                xsend[p, i // 2, i % 2] = core_sum(p, i).astype(BF16)
                if i % 2 == 1:
                    x_copy(p, i // 2).start()

    def across_copy(p):
        return remote(fsend.at[p], frecv.at[p], fs_sem.at[p], fr_sem.at[p], across)

    def tail_y(p):
        for i in range(3):
            x_copy(p, i).wait_recv()
        for its_yh in range(2):
            total = core_sum(p, 6 + its_yh)
            for i in range(3):
                total = total + xrecv[p, i, its_yh].astype(F32)

            @pl.when(yh == its_yh)
            def _():
                kept[p] = total

            @pl.when(yh != its_yh)
            def _():
                fsend[p] = total.astype(BF16)
        across_copy(p).start()

    def tail_end(p):
        across_copy(p).wait_recv()
        at = slice(p * PIECE, (p + 1) * PIECE)
        output[at, :] = (kept[p, 0] + frecv[p, 0].astype(F32)).astype(BF16)
        grad_tokens[at, :] = (kept[p, 1] + frecv[p, 1].astype(F32)).astype(BF16)

    def last_copy(i):
        its_x, its_yh = ((xp, yh), (xm, yh), (xp, 1 - yh), (xm, 1 - yh), (xq, yh), (xq, 1 - yh), (x, 1 - yh))[i]
        return remote(lsend.at[i], lrecv.at[i], ls_sem.at[i], lr_sem.at[i], at_chip(its_x, its_yh))

    def last_slot(i):
        return ((0, yh), (1, yh), (0, 1 - yh), (1, 1 - yh), (2, yh), (2, 1 - yh), (3, 1 - yh), (3, yh))[i]

    def last_sum_of(i):
        its_x, its_yh = last_slot(i)
        place_x = (xp, xm, xq, x)[its_x]
        at = pl.ds(pl.multiple_of(place(place_x, its_yh) * slot_rows + core * PIECE, PIECE), PIECE)
        return acc[(PARTS - 1) % 2, :, at, :] + crecv[PARTS - 1, its_x * 2 + its_yh]

    def last_send():
        for i in range(8):
            tail_copy(PARTS - 1, i).wait_recv()
            if i % 2 == 1:
                for j in ((0, 2), (1, 3), (4, 5), (6,))[i // 2]:
                    lsend[j] = last_sum_of(j).astype(BF16)
                    last_copy(j).start()

    def last_sum():
        total = last_sum_of(7)
        for i in range(7):
            last_copy(i).wait_recv()
            total = total + lrecv[i].astype(F32)
        at = slice((PARTS - 1) * PIECE, PARTS * PIECE)
        output[at, :] = total[0].astype(BF16)
        grad_tokens[at, :] = total[1].astype(BF16)

    def grad_copies(k):
        cols = pl.ds(k * COLS, COLS) if isinstance(k, int) else pl.ds(pl.multiple_of(k * COLS, COLS), COLS)
        at = k % 2 if isinstance(k, int) else lax.rem(k, 2)
        return (
            pltpu.make_async_copy(gg.at[at], grad_gate.at[:, cols], g_sem.at[at, 0]),
            pltpu.make_async_copy(gu.at[at], grad_up.at[:, cols], g_sem.at[at, 1]),
            pltpu.make_async_copy(gd.at[at], grad_down.at[cols, :], g_sem.at[at, 2]),
        )

    def weight_grads(k):
        at = k % 2 if isinstance(k, int) else lax.rem(k, 2)

        @pl.when(k >= 2)
        def _():
            for copy in grad_copies(k - 2):
                copy.wait()

        def units(i):
            cols = slice(i * COLS, (i + 1) * COLS)
            return jnp.concatenate(
                [ag[p * nk + k, :, :, :, cols].reshape(rows, COLS) for p in range(PARTS)], axis=0
            )

        contract = (((0,), (0,)), ((), ()))
        hidden, d_gate, d_up = units(0), units(1), units(2)
        for n in range(4):
            cols = slice(n * 256, (n + 1) * 256)
            t = tok[:, :, :, :, cols].reshape(PARTS * rows, 256)
            for d, mask, out in ((d_gate, mg, gg), (d_up, mu, gu)):
                res = lax.dot_general(t, d, contract, preferred_element_type=F32)
                for r in range(2):
                    keep = jnp.broadcast_to(mask[k, 2 * n + r:2 * n + r + 1, :], (BLOCK, COLS))
                    kept_rows = jnp.where(keep > 0.0, res[r * BLOCK:(r + 1) * BLOCK], 0.0)
                    out[at, (2 * n + r) * BLOCK:(2 * n + r + 1) * BLOCK, :] = kept_rows.astype(BF16)
            g = grd[:, :, :, :, cols].reshape(PARTS * rows, 256)
            res = lax.dot_general(hidden, g, contract, preferred_element_type=F32)
            for i in range(blocks):
                row = md[pl.ds(blocks * k + i, 1), cols]
                keep = jnp.broadcast_to(row, (BLOCK, 256))
                kept_rows = jnp.where(keep > 0.0, res[i * BLOCK:(i + 1) * BLOCK], 0.0)
                gd[at, i * BLOCK:(i + 1) * BLOCK, cols] = kept_rows.astype(BF16)
        for copy in grad_copies(k):
            copy.start()

    lag = LAGS[-1]

    def step(t, carry):
        def run(offset, what):
            s = t - offset

            @pl.when((s >= 0) & (s < steps))
            def _():
                what(s)

        k = t - LAGS[-1] - 1 - (PARTS - 1) * nk

        @pl.when(k >= 0)
        def _():
            weight_grads(k)

        for offset, what in zip(LAGS, (partials, after_pair, activate, pass_partner, pass_on, back)):
            run(offset, what)

        for p in range(PARTS - 1):
            for after, what in enumerate((tail_pair, tail_x, tail_y, tail_end)):
                @pl.when(t == (p + 1) * nk - 1 + lag + after)
                def _():
                    what(p)
        return carry

    lax.fori_loop(0, steps + lag, step, 0)
    tail_pair(PARTS - 1)
    last_send()
    weight_grads(nk - 1)
    last_sum()

    def drain(s, carry):
        @pl.when(s > 0)
        def _():
            remote(ysend.at[s], yrecv.at[s], ys_sem.at[s], yr_sem.at[s], partner).wait_send()
        for i in range(3):
            remote(zsend.at[s, i], zrecv.at[s, i], zs_sem.at[s, i], zr_sem.at[s, i], partner).wait_send()
        for i in range(7):
            ag_copy(s, i).wait_send()
        return carry

    lax.fori_loop(0, steps, drain, 0)
    for i in range(2):
        first_copy(i).wait_send()
    for p in range(PARTS):
        for a in range(2):
            for i in range(15):
                gather_copy(p, a, i).wait_send()
        if p > 0:
            for i in range(8):
                tail_copy(p, i).wait_send()
        if p < PARTS - 1:
            for i in range(3):
                x_copy(p, i).wait_send()
            across_copy(p).wait_send()
    for i in range(7):
        last_copy(i).wait_send()
    for k in (nk - 2, nk - 1):
        for copy in grad_copies(k):
            copy.wait()


def layer(tokens, gate_w, up_w, down_w, grad_out, pat_gate, pat_up, pat_down):
    rows, width = tokens.shape
    hidden = gate_w.shape[1]
    nk = hidden // COLS
    steps = PARTS * nk
    any_, vmem = pl.BlockSpec(memory_space=pl.ANY), pl.BlockSpec(memory_space=pltpu.VMEM)
    dma, three, slot_rows = pltpu.SemaphoreType.DMA, 3 * COLS, 2 * PIECE
    small = jax.ShapeDtypeStruct((rows, width), BF16)
    whole = (PARTS, 8, 2, PIECE, width)
    return pl.pallas_call(
        functools.partial(layer_kernel, nk),
        name="layer",
        out_shape=(
            small, small,
            jax.ShapeDtypeStruct((width, hidden), BF16),
            jax.ShapeDtypeStruct((width, hidden), BF16),
            jax.ShapeDtypeStruct((hidden, width), BF16),
        ),
        in_specs=[any_] * 5 + [vmem] * 3,
        out_specs=(vmem, vmem, any_, any_, any_),
        scratch_shapes=[
            pltpu.VMEM((nk, width, COLS), BF16),
            pltpu.VMEM((nk, width, COLS), BF16),
            pltpu.VMEM((nk, COLS, width), BF16),
            pltpu.VMEM((nk, 8, COLS), F32),
            pltpu.VMEM((nk, 8, COLS), F32),
            pltpu.VMEM((hidden // BLOCK, width), F32),
            pltpu.VMEM(whole, BF16),
            pltpu.VMEM(whole, BF16),
            pltpu.VMEM((SLOTS, 4, slot_rows, three), F32),
            pltpu.VMEM((steps, 4, slot_rows, three), BF16),
            pltpu.VMEM((steps, 4, slot_rows, three), BF16),
            pltpu.VMEM((steps, 3, slot_rows, three), BF16),
            pltpu.VMEM((steps, 3, slot_rows, three), BF16),
            pltpu.VMEM((steps, 2, 4, slot_rows, three), BF16),
            pltpu.VMEM((2, 2, 16 * PIECE, width), F32),
            pltpu.VMEM((PARTS, 8, 2, PIECE, width), F32),
            pltpu.VMEM((PARTS, 3, 2, 2, PIECE, width), BF16),
            pltpu.VMEM((PARTS, 3, 2, 2, PIECE, width), BF16),
            pltpu.VMEM((PARTS, 2, PIECE, width), F32),
            pltpu.VMEM((PARTS, 2, PIECE, width), BF16),
            pltpu.VMEM((PARTS, 2, PIECE, width), BF16),
            pltpu.VMEM((2, width, COLS), BF16),
            pltpu.VMEM((2, width, COLS), BF16),
            pltpu.VMEM((2, COLS, width), BF16),
            pltpu.VMEM((7, 2, PIECE, width), BF16),
            pltpu.VMEM((7, 2, PIECE, width), BF16),
            dma((3, nk)), dma((2, PARTS)), dma((PARTS, 2, 15)), dma((PARTS, 2, 15)),
            dma((steps,)), dma((steps,)), dma((steps, 3)), dma((steps, 3)),
            dma((steps, 7)), dma((steps, 7)), dma((PARTS, 8)), dma((PARTS, 8)),
            dma((PARTS, 3)), dma((PARTS, 3)), dma((PARTS,)), dma((PARTS,)),
            dma((2, 3)), dma((7,)), dma((7,)), dma((4,)),
        ],
        compiler_params=pltpu.CompilerParams(
            collective_id=0, has_side_effects=True, vmem_limit_bytes=60 * 2**20
        ),
    )(tokens, gate_w, up_w, down_w, grad_out, pat_gate, pat_up, pat_down)


def hand_out_kernel(*refs):
    n = len(refs) // 2
    for src, dst in zip(refs[:n], refs[n:]):
        dst[...] = src[...]


def hand_out(*arrays):
    specs = tuple(pl.BlockSpec((a.shape[0] // CUTS, a.shape[1]), lambda i: (i, 0)) for a in arrays)
    return pl.pallas_call(
        hand_out_kernel,
        name="hand_out",
        grid=(CUTS,),
        out_shape=tuple(jax.ShapeDtypeStruct(a.shape, a.dtype) for a in arrays),
        in_specs=list(specs),
        out_specs=specs,
        compiler_params=pltpu.CompilerParams(vmem_limit_bytes=60 * 2**20),
    )(*arrays)


def per_device(*args):
    output, grad_tokens, *grads = layer(*args)
    return output, grad_tokens, *hand_out(*grads)


def solution(mesh):
    placed = (
        P("hidden", "width"),
        P("width", "hidden"),
        P("width", "hidden"),
        P("hidden", "width"),
        P("hidden", "width"),
        P("width", None),
        P("width", None),
        P("hidden", None),
    )
    return jax.shard_map(
        per_device,
        mesh=mesh,
        in_specs=placed,
        out_specs=(
            P("hidden", "width"),
            P("hidden", "width"),
            P("width", "hidden"),
            P("width", "hidden"),
            P("hidden", "width"),
        ),
        check_vma=False,
    )
```

time: 591 us -> 183 us (0.31)
  waiting for transfers between devices: 439 us -> 0 us
  Pallas kernels: 0 us -> 180 us
  matrix products: 64 us -> 0 us
  local copies, waits for them, and re-layouts: 48.8 us -> 1.29 us
  other arithmetic: 23.1 us -> 0 us
  between operations: 13.9 us -> 0.66 us
    reduce_scatter x4 -> x0, waiting for transfers between devices: 269 us -> none  [the longest x1 119 us: per_device(): lax.psum_scatter(jnp.concatenate([jnp.dot(picked, w_gate, preferred_eleme...]
    pallas_call x0 -> x2, Pallas kernels: none -> 180 us  [the longest x1 170 us: layer(): pl.pallas_call(functools.partial(layer_kernel, nk), name='layer', out_sha...]
    all_gather x5 -> x0, waiting for transfers between devices: 168 us -> none  [the longest x1 50.9 us: per_device(): grad_all = lax.all_gather(grad_out, 'hidden', axis=0, tiled=True)]
    dot_general x9 -> x0, matrix products: 64 us -> none  [the longest x1 8.44 us: per_device(): lax.dot_general(d_up_all, w_up, back, preferred_element_type=jnp.float32)]
    unnamed x23 -> x6, local copies, waits for them, and re-layouts: 43.1 us -> 1.29 us
    concatenate x1 -> x0, other arithmetic: 9.08 us -> none  [per_device(): jnp.concatenate([jnp.dot(picked, w_gate, preferred_element_type=jnp.float...]
    select_n x2 -> x0, other arithmetic: 6.41 us -> none  [the longest x1 4.3 us: per_device(): w_up = jnp.where(mask_up, up_weight, zero)]
    convert_element_type x3 -> x0, other arithmetic: 5.92 us -> none  [the longest x1 2.77 us: per_device(): d_up = (grad_hidden * gate * sig).astype(jnp.bfloat16)]
  transfers between devices with their start and end apart: 9 -> 0, of which waited for: 9 -> 0; matrix products, arithmetic and copies ran while one was open for 22% -> 0% of each run, Pallas kernels for 0% -> 0%
where the time goes in v2:
time: 183 us; the launch traced here: 182 us
  Pallas kernels  180 us (98%)
    pallas_call x1, Pallas kernels, layer(): pl.pallas_call(functools.partial(layer_kernel, nk), name='layer', out_sha...  170 us
    pallas_call x1, Pallas kernels, hand_out(): pl.pallas_call(hand_out_kernel, name='hand_out', grid=(CUTS,), out_shape=...  10.4 us

profile of v2, /device:TPU:1, one launch (start us, length us, event | category | flops | bytes accessed | tf_op | source)
XLA Modules:
  0.0 182.3 jit_solution(926517375186561864)
XLA Ops:
  0.6 169.9 %layer.1 = (bf16[48,1024]{1,0:T(8,128)(2,1)}, bf16[48,1024]{1,0:T(8,128)(2,1)}, bf16[1024,1792]{1,0:T(8,128)(2,1)}, bf16[1024,1792]{1,0:T(8,128)(2,1)}, bf16[1792,1024]{1,0:T(8,128)(2,1)}) custom-call(bf16[48,1024]{1,0:T(8,128)(2,1)} %tokens.1, bf16[1024,1792]{1,0:T(8,128)(2,1)} %gate_w.1, bf16[1024,1792]{1,0:T(8,128)(2,1)} %up_w.1, ...), custom_call_target="tpu_custom_call" | custom-call | tf_op jit(solution)/shard_map/layer/pallas_call | solution.py:539
  170.6 0.0 copy-start.1
  170.6 0.0 copy-start
  170.6 10.4 %hand_out.1 = (bf16[1024,1792]{1,0:T(8,128)(2,1)}, bf16[1024,1792]{1,0:T(8,128)(2,1)}, bf16[1792,1024]{1,0:T(8,128)(2,1)}) custom-call(bf16[1024,1792]{1,0:T(8,128)(2,1)} %get-tuple-element.15.refs_0_, bf16[1024,1792]{1,0:T(8,128)(2,1)} %get-tuple-element.16.refs_1_, bf16[1792,1024]{1,0:T(8,128)(2,1)} %get-tuple-element.17.refs_2_), custom_call_target="tpu_custom_call" | custom-call | tf_op jit(solution)/shard_map/hand_out/pallas_call | solution.py:597
  181.0 0.0 copy-done.1
  181.0 0.6 copy.15
  181.6 0.0 copy-done
  181.6 0.6 copy.16
Async XLA Ops:
  170.6 10.4 %copy-start.1 = (bf16[48,1024]{1,0:T(8,128)(2,1)S(1)}, bf16[48,1024]{1,0:T(8,128)(2,1)}, u32[]{:S(2)}) copy-start(bf16[48,1024]{1,0:T(8,128)(2,1)} %get-tuple-element.26) | copy-start | bytes 294916
  170.6 11.0 %copy-start = (bf16[48,1024]{1,0:T(8,128)(2,1)S(1)}, bf16[48,1024]{1,0:T(8,128)(2,1)}, u32[]{:S(2)}) copy-start(bf16[48,1024]{1,0:T(8,128)(2,1)} %get-tuple-element.27) | copy-start | bytes 294916

commit v3 on v2

--- a/solution.py
+++ b/solution.py
@@ -14,7 +14,7 @@
 LAGS = (0, 1, 2, 3, 4, 5)
 SLOTS = 4
 DIRECT = 1
-CUTS = 8
+CUTS = 4
 MESH = pl.DeviceIdType.MESH
 F32 = jnp.float32
 BF16 = jnp.bfloat16
@@ -38,7 +38,7 @@
     wg, wu, wd, mg, mu, md, tok, grd, own, ysend, yrecv, zsend, zrecv, ag, acc,
     crecv, xsend, xrecv, kept, fsend, frecv, gg, gu, gd, lsend, lrecv,
     w_sem, o_sem, hs_sem, hr_sem, ys_sem, yr_sem, zs_sem, zr_sem,
-    as_sem, ar_sem, cs_sem, cr_sem, xs_sem, xr_sem, fs_sem, fr_sem, g_sem, ls_sem, lr_sem, y0_sem,
+    as_sem, ar_sem, cs_sem, cr_sem, xs_sem, xr_sem, fs_sem, fr_sem, g_sem, ls_sem, lr_sem, y0_sem, yd_sem,
 ):
     steps = PARTS * nk
     width = lax.axis_index("width")
@@ -123,9 +123,14 @@
         dst = gathered(p, a, i)
         remote(dst, dst, hs_sem.at[p, a, i], hr_sem.at[p, a, i], sibling).wait_recv()
 
+    def gather_early(p, a):
+        own_copy(p, a).wait()
+        gather_copy(p, a, 1).start()
+
     def gather_send(p, a):
-        own_copy(p, a).wait()
-        for i in (1, 5, 6, 7, 2, 3, 4, 0) if p == 0 else (1, 2, 3, 4, 0):
+        if p == 0:
+            own_copy(p, a).wait()
+        for i in (1, 5, 6, 7, 2, 3, 4, 0) if p == 0 else (2, 3, 4, 0):
             gather_copy(p, a, i).start()
 
     def gather_across(p, a):
@@ -147,6 +152,9 @@
     for k in range(1, nk):
         for copy in weight_copies(k):
             copy.start()
+    for p in range(1, PARTS):
+        for a in range(2):
+            gather_early(p, a)
 
     blocks = COLS // BLOCK
     for b in range(nk * blocks):
@@ -180,6 +188,19 @@
             keep = jnp.broadcast_to(row, (BLOCK, row.shape[1])).astype(BF16)
             wd[k, at, :] = wd[k, at, :] * keep
 
+    def z_copy(s, i):
+        return remote(zsend.at[s, i], zrecv.at[s, i], zs_sem.at[s, i], zr_sem.at[s, i], at_z((zq, zp, zm)[i]))
+
+    def straight_copy(i):
+        to = (zq, zp, zm, z)[i]
+        return remote(
+            ysend.at[steps - 1, to], yrecv.at[steps - 1, z], yd_sem.at[i], yd_sem.at[4 + i], other_y(to)
+        )
+
+    def straight_wait(i):
+        src = yrecv.at[steps - 1, (zq, zm, zp, z)[i]]
+        remote(src, src, yd_sem.at[i], yd_sem.at[4 + i], partner).wait_recv()
+
     def first_copy(i):
         cols = (pl.ds(0, 2 * COLS), pl.ds(2 * COLS, COLS))[i]
         return remote(ysend.at[0, :, :, cols], yrecv.at[0, :, :, cols], y0_sem.at[i], y0_sem.at[2 + i], partner)
@@ -225,9 +246,17 @@
         def _():
             first_copy(1).start()
 
-        @pl.when(s > 0)
+        @pl.when((s > 0) & (s < steps - 1))
         def _():
             remote(ysend.at[s], yrecv.at[s], ys_sem.at[s], yr_sem.at[s], partner).start()
+
+        @pl.when(s == steps - 1)
+        def _():
+            for i in range(4):
+                straight_copy(i).start()
+            for i, to in enumerate((zq, zp, zm)):
+                zsend[s, i] = own[slot, to].astype(BF16)
+                z_copy(s, i).start()
 
         for p in range(1, PARTS):
             for at, what in ((0, gather_send), (2, gather_across), (4, gather_share)):
@@ -245,12 +274,15 @@
             for i in range(2):
                 first_copy(i).wait_recv()
 
-        @pl.when(s > 0)
+        @pl.when((s > 0) & (s < steps - 1))
         def _():
             remote(ysend.at[s], yrecv.at[s], ys_sem.at[s], yr_sem.at[s], partner).wait_recv()
-        for i, to in enumerate((zp, zm, zq)):
-            zsend[s, i] = pair_sum(s, to).astype(BF16)
-            remote(zsend.at[s, i], zrecv.at[s, i], zs_sem.at[s, i], zr_sem.at[s, i], at_z(to)).start()
+
+        @pl.when(s < steps - 1)
+        def _():
+            for i, to in enumerate((zq, zp, zm)):
+                zsend[s, i] = pair_sum(s, to).astype(BF16)
+                z_copy(s, i).start()
 
     def ag_copy(s, i):
         src, to = (
@@ -273,8 +305,16 @@
         remote(here, here, as_sem.at[s, i], ar_sem.at[s, i], partner).wait_recv()
 
     def activate(s):
+        at = lax.rem(s, SLOTS)
+
+        @pl.when(s == steps - 1)
+        def _():
+            for i in range(4):
+                straight_wait(i)
+            for to in (zq, zp, zm):
+                own[at, z] += yrecv[s, to].astype(F32)
         for i in range(3):
-            remote(zsend.at[s, i], zrecv.at[s, i], zs_sem.at[s, i], zr_sem.at[s, i], at_z(zp)).wait_recv()
+            z_copy(s, i).wait_recv()
         total = pair_sum(s, z)
         for i in range(3):
             total = total + zrecv[s, i].astype(F32)
@@ -497,11 +537,11 @@
     last_sum()
 
     def drain(s, carry):
-        @pl.when(s > 0)
+        @pl.when((s > 0) & (s < steps - 1))
         def _():
             remote(ysend.at[s], yrecv.at[s], ys_sem.at[s], yr_sem.at[s], partner).wait_send()
         for i in range(3):
-            remote(zsend.at[s, i], zrecv.at[s, i], zs_sem.at[s, i], zr_sem.at[s, i], partner).wait_send()
+            z_copy(s, i).wait_send()
         for i in range(7):
             ag_copy(s, i).wait_send()
         return carry
@@ -509,6 +549,8 @@
     lax.fori_loop(0, steps, drain, 0)
     for i in range(2):
         first_copy(i).wait_send()
+    for i in range(4):
+        straight_copy(i).wait_send()
     for p in range(PARTS):
         for a in range(2):
             for i in range(15):
@@ -578,7 +620,7 @@
             dma((steps,)), dma((steps,)), dma((steps, 3)), dma((steps, 3)),
             dma((steps, 7)), dma((steps, 7)), dma((PARTS, 8)), dma((PARTS, 8)),
             dma((PARTS, 3)), dma((PARTS, 3)), dma((PARTS,)), dma((PARTS,)),
-            dma((2, 3)), dma((7,)), dma((7,)), dma((4,)),
+            dma((2, 3)), dma((7,)), dma((7,)), dma((4,)), dma((8,)),
         ],
         compiler_params=pltpu.CompilerParams(
             collective_id=0, has_side_effects=True, vmem_limit_bytes=60 * 2**20
@@ -587,27 +629,48 @@
 
 
 def hand_out_kernel(*refs):
-    n = len(refs) // 2
-    for src, dst in zip(refs[:n], refs[n:]):
-        dst[...] = src[...]
+    n = (len(refs) - 2) // 3
+    reads, writes = refs[-2:]
+    pieces = []
+    for a in range(n):
+        src, dst, held = refs[a], refs[n + a], refs[2 * n + a]
+        cuts = CUTS if src.shape[0] >= 256 else 1
+        size = src.shape[0] // cuts
+        for c in range(cuts):
+            at = pl.ds(c * size, size)
+            pieces.append((
+                pltpu.make_async_copy(src.at[at], held.at[at], reads.at[a, c]),
+                pltpu.make_async_copy(held.at[at], dst.at[at], writes.at[a, c]),
+            ))
+    for read, _ in pieces:
+        read.start()
+    for read, write in pieces:
+        read.wait()
+        write.start()
+    for _, write in pieces:
+        write.wait()
 
 
 def hand_out(*arrays):
-    specs = tuple(pl.BlockSpec((a.shape[0] // CUTS, a.shape[1]), lambda i: (i, 0)) for a in arrays)
+    any_ = pl.BlockSpec(memory_space=pl.ANY)
+    n = len(arrays)
     return pl.pallas_call(
         hand_out_kernel,
         name="hand_out",
-        grid=(CUTS,),
         out_shape=tuple(jax.ShapeDtypeStruct(a.shape, a.dtype) for a in arrays),
-        in_specs=list(specs),
-        out_specs=specs,
+        in_specs=[any_] * n,
+        out_specs=(any_,) * n,
+        scratch_shapes=[pltpu.VMEM(a.shape, a.dtype) for a in arrays]
+        + [pltpu.SemaphoreType.DMA((n, CUTS)), pltpu.SemaphoreType.DMA((n, CUTS))],
         compiler_params=pltpu.CompilerParams(vmem_limit_bytes=60 * 2**20),
+        cost_estimate=pl.CostEstimate(
+            flops=0, bytes_accessed=sum(4 * a.size for a in arrays), transcendentals=0
+        ),
     )(*arrays)
 
 
 def per_device(*args):
-    output, grad_tokens, *grads = layer(*args)
-    return output, grad_tokens, *hand_out(*grads)
+    return hand_out(*layer(*args))
 
 
 def solution(mesh):

time: 183 us -> 179 us (0.978)
  Pallas kernels: 180 us -> 178 us
where the time goes in v3:
time: 179 us
  Pallas kernels  178 us (99%)
    pallas_call x1, Pallas kernels, layer(): pl.pallas_call(functools.partial(layer_kernel, nk), name='layer', out_sha...  169 us
    pallas_call x1, Pallas kernels, hand_out(): pl.pallas_call(hand_out_kernel, name='hand_out', out_shape=tuple((jax.Sha...  8.91 us

profile of v3, /device:TPU:1, one launch (start us, length us, event | category | flops | bytes accessed | tf_op | source)
XLA Modules:
  0.0 178.8 jit_solution(12799641113768291550)
XLA Ops:
  0.6 169.3 %layer.1 = (bf16[48,1024]{1,0:T(8,128)(2,1)}, bf16[48,1024]{1,0:T(8,128)(2,1)}, bf16[1024,1792]{1,0:T(8,128)(2,1)}, bf16[1024,1792]{1,0:T(8,128)(2,1)}, bf16[1792,1024]{1,0:T(8,128)(2,1)}) custom-call(bf16[48,1024]{1,0:T(8,128)(2,1)} %tokens.1, bf16[1024,1792]{1,0:T(8,128)(2,1)} %gate_w.1, bf16[1024,1792]{1,0:T(8,128)(2,1)} %up_w.1, ...), custom_call_target="tpu_custom_call" | custom-call | tf_op jit(solution)/shard_map/layer/pallas_call | solution.py:581
  169.9 8.9 %hand_out.1 = (bf16[48,1024]{1,0:T(8,128)(2,1)}, bf16[48,1024]{1,0:T(8,128)(2,1)}, bf16[1024,1792]{1,0:T(8,128)(2,1)}, bf16[1024,1792]{1,0:T(8,128)(2,1)}, bf16[1792,1024]{1,0:T(8,128)(2,1)}) custom-call(bf16[48,1024]{1,0:T(8,128)(2,1)} %get-tuple-element.10.refs_0_, bf16[48,1024]{1,0:T(8,128)(2,1)} %get-tuple-element.11.refs_1_, ...), custom_call_target="tpu_custom_call" | custom-call | bytes 22413312 | tf_op jit(solution)/shard_map/hand_out/pallas_call | solution.py:657

commit v4 on v3

--- a/solution.py
+++ b/solution.py
@@ -13,6 +13,7 @@
 PIECE = 16
 LAGS = (0, 1, 2, 3, 4, 5)
 SLOTS = 4
+LATE = 2
 DIRECT = 1
 CUTS = 4
 MESH = pl.DeviceIdType.MESH
@@ -516,7 +517,7 @@
 
         k = t - LAGS[-1] - 1 - (PARTS - 1) * nk
 
-        @pl.when(k >= 0)
+        @pl.when((k >= 0) & (k < nk - LATE))
         def _():
             weight_grads(k)
 
@@ -533,7 +534,8 @@
     lax.fori_loop(0, steps + lag, step, 0)
     tail_pair(PARTS - 1)
     last_send()
-    weight_grads(nk - 1)
+    for k in range(nk - LATE, nk):
+        weight_grads(k)
     last_sum()
 
     def drain(s, carry):

time: 179 us -> 178 us (level)
  no operation moved by 1% of the time
where the time goes in v4:
time: 178 us; the launch traced here: 177 us
  Pallas kernels  177 us (99%)
    pallas_call x1, Pallas kernels, layer(): pl.pallas_call(functools.partial(layer_kernel, nk), name='layer', out_sha...  168 us
    pallas_call x1, Pallas kernels, hand_out(): pl.pallas_call(hand_out_kernel, name='hand_out', out_shape=tuple((jax.Sha...  8.91 us

profile of v4, /device:TPU:1, one launch (start us, length us, event | category | flops | bytes accessed | tf_op | source)
XLA Modules:
  0.0 177.4 jit_solution(14031032376813549337)
XLA Ops:
  0.6 167.8 %layer.1 = (bf16[48,1024]{1,0:T(8,128)(2,1)}, bf16[48,1024]{1,0:T(8,128)(2,1)}, bf16[1024,1792]{1,0:T(8,128)(2,1)}, bf16[1024,1792]{1,0:T(8,128)(2,1)}, bf16[1792,1024]{1,0:T(8,128)(2,1)}) custom-call(bf16[48,1024]{1,0:T(8,128)(2,1)} %tokens.1, bf16[1024,1792]{1,0:T(8,128)(2,1)} %gate_w.1, bf16[1024,1792]{1,0:T(8,128)(2,1)} %up_w.1, ...), custom_call_target="tpu_custom_call" | custom-call | tf_op jit(solution)/shard_map/layer/pallas_call | solution.py:583
  168.5 8.9 %hand_out.1 = (bf16[48,1024]{1,0:T(8,128)(2,1)}, bf16[48,1024]{1,0:T(8,128)(2,1)}, bf16[1024,1792]{1,0:T(8,128)(2,1)}, bf16[1024,1792]{1,0:T(8,128)(2,1)}, bf16[1792,1024]{1,0:T(8,128)(2,1)}) custom-call(bf16[48,1024]{1,0:T(8,128)(2,1)} %get-tuple-element.10.refs_0_, bf16[48,1024]{1,0:T(8,128)(2,1)} %get-tuple-element.11.refs_1_, ...), custom_call_target="tpu_custom_call" | custom-call | bytes 22413312 | tf_op jit(solution)/shard_map/hand_out/pallas_call | solution.py:659

commit v5 on v4

--- a/solution.py
+++ b/solution.py
@@ -15,7 +15,7 @@
 SLOTS = 4
 LATE = 2
 DIRECT = 1
-CUTS = 4
+CUTS = 2
 MESH = pl.DeviceIdType.MESH
 F32 = jnp.float32
 BF16 = jnp.bfloat16
@@ -631,43 +631,26 @@
 
 
 def hand_out_kernel(*refs):
-    n = (len(refs) - 2) // 3
-    reads, writes = refs[-2:]
-    pieces = []
-    for a in range(n):
-        src, dst, held = refs[a], refs[n + a], refs[2 * n + a]
-        cuts = CUTS if src.shape[0] >= 256 else 1
-        size = src.shape[0] // cuts
-        for c in range(cuts):
-            at = pl.ds(c * size, size)
-            pieces.append((
-                pltpu.make_async_copy(src.at[at], held.at[at], reads.at[a, c]),
-                pltpu.make_async_copy(held.at[at], dst.at[at], writes.at[a, c]),
-            ))
-    for read, _ in pieces:
-        read.start()
-    for read, write in pieces:
-        read.wait()
-        write.start()
-    for _, write in pieces:
-        write.wait()
+    n = len(refs) // 2
+    for src, dst in zip(refs[:n], refs[n:]):
+        dst[...] = src[...]
 
 
 def hand_out(*arrays):
-    any_ = pl.BlockSpec(memory_space=pl.ANY)
-    n = len(arrays)
+    def block(a):
+        if a.shape[0] < 256:
+            return pl.BlockSpec(a.shape, lambda i: (0, 0))
+        return pl.BlockSpec((a.shape[0] // CUTS, a.shape[1]), lambda i: (i, 0))
+
+    specs = tuple(block(a) for a in arrays)
     return pl.pallas_call(
         hand_out_kernel,
         name="hand_out",
+        grid=(CUTS,),
         out_shape=tuple(jax.ShapeDtypeStruct(a.shape, a.dtype) for a in arrays),
-        in_specs=[any_] * n,
-        out_specs=(any_,) * n,
-        scratch_shapes=[pltpu.VMEM(a.shape, a.dtype) for a in arrays]
-        + [pltpu.SemaphoreType.DMA((n, CUTS)), pltpu.SemaphoreType.DMA((n, CUTS))],
+        in_specs=list(specs),
+        out_specs=specs,
         compiler_params=pltpu.CompilerParams(vmem_limit_bytes=60 * 2**20),
-        cost_estimate=pl.CostEstimate(
-            flops=0, bytes_accessed=sum(4 * a.size for a in arrays), transcendentals=0
-        ),
     )(*arrays)
 
 

time: 178 us -> 176 us (0.989)
  Pallas kernels: 177 us -> 175 us
where the time goes in v5:
time: 176 us
  Pallas kernels  175 us (99%)
    pallas_call x1, Pallas kernels, layer(): pl.pallas_call(functools.partial(layer_kernel, nk), name='layer', out_sha...  168 us
    pallas_call x1, Pallas kernels, hand_out(): pl.pallas_call(hand_out_kernel, name='hand_out', grid=(CUTS,), out_shape=...  7.43 us

profile of v5, /device:TPU:1, one launch (start us, length us, event | category | flops | bytes accessed | tf_op | source)
XLA Modules:
  0.0 175.9 jit_solution(2791440269011371139)
XLA Ops:
  0.6 167.8 %layer.1 = (bf16[48,1024]{1,0:T(8,128)(2,1)}, bf16[48,1024]{1,0:T(8,128)(2,1)}, bf16[1024,1792]{1,0:T(8,128)(2,1)}, bf16[1024,1792]{1,0:T(8,128)(2,1)}, bf16[1792,1024]{1,0:T(8,128)(2,1)}) custom-call(bf16[48,1024]{1,0:T(8,128)(2,1)} %tokens.1, bf16[1024,1792]{1,0:T(8,128)(2,1)} %gate_w.1, bf16[1024,1792]{1,0:T(8,128)(2,1)} %up_w.1, ...), custom_call_target="tpu_custom_call" | custom-call | tf_op jit(solution)/shard_map/layer/pallas_call | solution.py:583
  168.5 7.4 %hand_out.1 = (bf16[48,1024]{1,0:T(8,128)(2,1)}, bf16[48,1024]{1,0:T(8,128)(2,1)}, bf16[1024,1792]{1,0:T(8,128)(2,1)}, bf16[1024,1792]{1,0:T(8,128)(2,1)}, bf16[1792,1024]{1,0:T(8,128)(2,1)}) custom-call(bf16[48,1024]{1,0:T(8,128)(2,1)} %get-tuple-element.10.refs_0_, bf16[48,1024]{1,0:T(8,128)(2,1)} %get-tuple-element.11.refs_1_, ...), custom_call_target="tpu_custom_call" | custom-call | tf_op jit(solution)/shard_map/hand_out/pallas_call | solution.py:646
